TPU v7x, 512 devices: a whole 4x4x16 slice. The times are simulated.
512 devices in a mesh: slab: 128 (over z, y, core), sub: 4 (over x).
Axes of the slice: x: 4, y: 4, z: 16, core: 2. Of those that a mesh axis runs over, the one named last changes fastest.
Arguments:
- features: bfloat16 [4096, 128, 512], P('slab', 'sub'), may hold values from -6 to 6
- cotangent: bfloat16 [4096, 128, 512], P('slab', 'sub'), may hold values from -6 to 6
- weight: bfloat16 [64, 1728], replicated, may hold values from -0.15625 to 0.15625
- occupancy: int32 [512, 16], P('slab', 'sub'), may hold values from 0 to 1, as said below
Outputs:
- out_features: bfloat16 [4096, 128, 512], P('slab', 'sub')
- in_grad: bfloat16 [4096, 128, 512], P('slab', 'sub')
- weight_grad: float32 [64, 1728], replicated
Inputs may be any that keep to these rules, and one draw needn't show every extreme that they name: `occupancy`: 1 marks an occupied brick, 0 an empty one. Every aligned block of 4 x 4 brick slots holds at least one occupied brick.
All inputs are finite; a program needn't handle non-finite values.
Results may differ from a plain program's by a relative error of at most 0.001.
Values may be sent and summed in bfloat16 or wider, within the bound.
A program may use at most 128 MiB of HBM per device.

v0:
```python
import jax
import jax.numpy as jnp
from jax import lax
from jax.sharding import PartitionSpec as P

C = 64
BRICK = 8
TAPS = 27
BZ = 4
BY = 4


def with_halo(array, sides, width):
    for axis, dim in sides:
        size, length = (lax.axis_size(axis), array.shape[dim])
        up = [(i, (i + 1) % size) for i in range(size - 1)]
        down = [(j, i) for i, j in up]
        last = lax.slice_in_dim(array, length - width, length, axis=dim)
        initial = lax.slice_in_dim(array, 0, width, axis=dim)
        before = lax.ppermute(last, axis, up)
        after = lax.ppermute(initial, axis, down)
        array = jnp.concatenate([before, array, after], axis=dim)
    return array


def tap_columns(grid_cells):
    columns = []
    for shift_z in range(3):
        for shift_y in range(3):
            for shift_x in range(3):
                window = grid_cells[
                    shift_z : shift_z + BRICK,
                    shift_y : shift_y + BRICK,
                    shift_x : shift_x + BRICK,
                    :,
                ]
                columns.append(window.reshape(-1, C))
    return jnp.concatenate(columns, axis=1)


def brick_terms(flat_pair, weight, weight_back):
    pair_cells = flat_pair.reshape(2, BRICK + 2, BRICK + 2, BRICK + 2, C)
    input_cols = tap_columns(pair_cells[0])
    grad_cols = tap_columns(pair_cells[1])
    output = lax.dot_general(
        input_cols, weight, (((1,), (1,)), ((), ())), preferred_element_type=jnp.float32
    )
    input_grad = jnp.dot(grad_cols, weight_back, preferred_element_type=jnp.float32)
    center = pair_cells[1, 1 : BRICK + 1, 1 : BRICK + 1, 1 : BRICK + 1, :].reshape(-1, C)
    weight_term = lax.dot_general(
        center, input_cols, (((0,), (0,)), ((), ())), preferred_element_type=jnp.float32
    )
    return (jnp.stack([output, input_grad]).astype(jnp.bfloat16), weight_term)


def convolve_list(brick_items, live_count, weight, weight_back):
    slot_total = brick_items.shape[0]
    results = jnp.zeros((slot_total, 2, BRICK**3, C), jnp.bfloat16)
    weight_sum = jnp.zeros(weight.shape, jnp.float32)

    def advance(item_index, state_pair):
        results, weight_sum = state_pair
        current = lax.dynamic_index_in_dim(brick_items, item_index, 0, keepdims=False)
        pair_out, weight_term = brick_terms(current, weight, weight_back)
        results = lax.dynamic_update_index_in_dim(results, pair_out, item_index, 0)
        return (results, weight_sum + weight_term)

    return lax.fori_loop(0, live_count, advance, (results, weight_sum))


def selector(targets, row_count):
    return (targets[None, :] == jnp.arange(row_count, dtype=jnp.int32)[:, None]).astype(
        jnp.bfloat16
    )


def select_rows(matrix, values):
    return jnp.dot(matrix, values, preferred_element_type=jnp.float32).astype(jnp.bfloat16)


def per_device(features, cotangent, weight, occupancy):
    slot_total = BZ * BY
    voxel_live = jnp.repeat(jnp.repeat(occupancy, BRICK, 0), BRICK, 1).astype(jnp.bfloat16)
    masked_in = features * voxel_live[:, :, None]
    masked_grad = cotangent * voxel_live[:, :, None]
    stacked = jnp.stack([masked_in, masked_grad])
    haloed = with_halo(stacked, (("slab", 1), ("sub", 2)), 1)
    grid_cells = haloed.reshape(2, BZ * BRICK + 2, BY * BRICK + 2, BRICK, C)
    grid_cells = jnp.pad(grid_cells, ((0, 0), (0, 0), (0, 0), (1, 1), (0, 0)))
    pieces = []
    for brick_z in range(BZ):
        for brick_y in range(BY):
            piece_cells = grid_cells[
                :,
                brick_z * BRICK : brick_z * BRICK + BRICK + 2,
                brick_y * BRICK : brick_y * BRICK + BRICK + 2,
            ]
            pieces.append(piece_cells.reshape(-1))
    brick_items = jnp.stack(pieces)
    weight_back = weight.reshape(C, TAPS, C)[:, ::-1, :].transpose(1, 0, 2).reshape(TAPS * C, C)
    live_flags = occupancy.reshape(-1)
    live_count = jnp.sum(live_flags)
    slot_ranks = jnp.cumsum(live_flags) - 1
    packer = selector(jnp.where(live_flags == 1, slot_ranks, -1), slot_total)
    packed = select_rows(packer, brick_items)
    results, weight_sum = convolve_list(packed, live_count, weight, weight_back)
    slot_out = select_rows(packer.T, results.reshape(slot_total, -1))
    grid_out = (
        slot_out.reshape(BZ, BY, 2, BRICK, BRICK, BRICK, C)
        .transpose(2, 0, 3, 1, 4, 5, 6)
        .reshape(2, BZ * BRICK, BY * BRICK, BRICK * C)
    )
    total_cells = lax.axis_size("slab") * lax.axis_size("sub") * slot_total * BRICK**3
    weight_grad = lax.psum(weight_sum, ("slab", "sub")) * total_cells ** (-0.5)
    return (grid_out[0], grid_out[1], weight_grad)


def solution(mesh):
    placed = (P("slab", "sub", None), P("slab", "sub", None), P(), P("slab", "sub"))
    return jax.shard_map(
        per_device,
        mesh=mesh,
        in_specs=placed,
        out_specs=(P("slab", "sub", None), P("slab", "sub", None), P()),
        check_vma=False,
    )
```

profile of v0, /device:TPU:1, one launch (start us, length us, event | category | flops | bytes accessed | tf_op | source)
XLA Modules:
  0.0 1057.3 jit_solution(5266541665975408491)
XLA Ops:
  10.9 4.6 collective-permute-start
  15.5 5.5 collective-permute-start.1
  36.9 4.3 reshape.276
  41.2 7.8 pad_slice_fusion
  83.2 23.9 %stack.24 = bf16[16,128000]{1,0:T(8,128)(2,1)} concatenate(bf16[1,128000]{1,0:T(2,128)(2,1)S(1)} %copy-done.2, bf16[1,128000]{1,0:T(2,128)(2,1)S(1)} %copy-done.3, bf16[1,128000]{1,0:T(2,128)(2,1)S(1)} %copy-done.4, bf16[1,128000]{1,0:T(2,128)(2,1)} %stack_reshape.51, bf16[1,128000]{1,0:T(2,128)(2,1)} %stack_reshape.52, bf16[1,128000]{1,0:T(2,128)(2,1)} %stack_reshape.53, ...), dimensions={0} | concatenate | bytes 8192000 | tf_op jit(solution)/shard_map/stack | solution.py:99
  107.1 5.3 convolution_convert_fusion.2
  114.0 171.9 %while.12 = (s32[]{:T(128)}, bf16[16,2,512,64]{2,3,1,0:T(8,128)(2,1)}, f32[64,1728]{1,0:T(8,128)S(1)}, s32[]{:T(128)}, bf16[16,128000]{1,0:T(8,128)(2,1)}, /*ind...) while((s32[]{:T(128)}, ...), condition=%wide.region_3.4_spmd, body=%wide.region_2.3_spmd.sunk | while | flops 340176896 | bytes 23429292 | solution.py:68
  121.1 4.1 concatenate.25
  130.5 5.1 concatenate.24
  149.6 4.1 concatenate.25
  159.0 5.1 concatenate.24
  178.1 4.1 concatenate.25
  187.5 5.1 concatenate.24
  206.6 4.1 concatenate.25
  216.0 5.1 concatenate.24
  235.1 4.1 concatenate.25
  244.5 5.1 concatenate.24
  263.6 4.1 concatenate.25
  273.0 5.1 concatenate.24
  285.9 4.9 copy.58
  290.9 4.7 reshape.279
  297.7 6.4 reshape.280
  304.1 4.7 fusion.8
  315.0 733.7 %all-reduce.3.cloned.1.call-done = f32[64,1728]{1,0:T(8,128)} async-done(((f32[64,1728]{1,0:T(8,128)}), f32[64,1728]{1,0:T(8,128)}) %all-reduce.3.cloned.1.call-update) | async-done | bytes 442384 | tf_op jit(solution)/shard_map/psum | solution.py:114
  (168 shorter events, 176.5 us)
Async XLA Ops:
  7.2 13.8 %copy-start.5 = (s32[4,4]{1,0:T(4,128)S(1)}, s32[4,4]{1,0:T(4,128)}, u32[]{:S(2)}) copy-start(s32[4,4]{1,0:T(4,128)} %param.9) | copy-start | bytes 196
  7.2 1041.5 %all-reduce.3.cloned.1.call-start = ((), (), s32[]{:S(2)}) async-start(), calls=%async_computation | async-start | bytes 917504 | tf_op jit(solution)/shard_map/psum | solution.py:114
  9.1 17.9 %copy-start.1 = (bf16[64,1728]{1,0:T(8,128)(2,1)S(1)}, bf16[64,1728]{1,0:T(8,128)(2,1)}, u32[]{:S(2)}) copy-start(bf16[64,1728]{1,0:T(8,128)(2,1)} %param.8) | copy-start | bytes 663556
  10.9 10.4 collective-permute-start
  15.5 6.4 collective-permute-start.1
  22.8 6.1 collective-permute-start.2
  25.1 7.3 collective-permute-start.3
  80.1 3.1 copy-start.2
  80.1 3.1 copy-start.3
  81.5 1.7 copy-start.4
  83.2 23.9 %copy-start.6 = (s32[16]{0:T(128)S(1)}, s32[16]{0:T(128)}, u32[]{:S(2)}) copy-start(s32[16]{0:T(128)} %broadcast_select_fusion) | copy-start | bytes 196
  285.9 9.7 copy-start
  290.9 4.7 copy-start.7
Sparse Core Ops, SparseCore 0:
  304.2 744.3 all-reduce.2
where the time goes:
time: 1070 us; the launch traced here: 1060 us
  waiting for transfers between devices  738 us (69%)
  local copies, waits for them, and re-layouts  240 us (22%)
  matrix products  33.2 us (3%)
  between operations  14.3 us (1%)
  starting transfers between devices  13.7 us (1%)
  other arithmetic  12.7 us (1%)
    psum x1, waiting for transfers between devices, per_device(): weight_grad = lax.psum(weight_sum, ('slab', 'sub')) * total_cells ** (-0.5)  734 us
    concatenate x12, local copies, waits for them, and re-layouts, tap_columns(): return jnp.concatenate(columns, axis=1)  55.1 us
    another operation x17, local copies, waits for them, and re-layouts, per_device(): brick_items = jnp.stack(pieces)  41.9 us
    slice x24, local copies, waits for them, and re-layouts, tap_columns(): grid_cells[shift_z:shift_z + BRICK, shift_y:shift_y + BRICK, shift_x:shif...  29.1 us
    slice x17, local copies, waits for them, and re-layouts, per_device(): grid_cells[:, brick_z * BRICK:brick_z * BRICK + BRICK + 2, brick_y * BRIC...  23.8 us
    slice x6, local copies, waits for them, and re-layouts, brick_terms(): input_cols = tap_columns(pair_cells[0])  23.1 us
  transfers between devices with their start and end apart: 5, of which 3 were waited for; matrix products, arithmetic and copies ran while one was open for 1% of the time, Pallas kernels for 0%

commit v1 on v0

v1 whole, which is shorter than its diff:
```python
import functools

import jax
import jax.numpy as jnp
from jax import lax
from jax.experimental import pallas as pl
from jax.experimental.pallas import tpu as pltpu
from jax.sharding import PartitionSpec as P

C = 64
BRICK = 8
ROWS = 32
XC = 512
PADX = XC + 2 * C
WINDOW = 384
TAPS = 27
MESH = pl.DeviceIdType.MESH
PLANE = 32
PIECES = 8
CHUNK = 512
WIDE = 4 * CHUNK

FACES_Z = ((1, 0), (-1, 0))
FACES_Y = ((0, 1), (0, -1))
CORNERS = ((1, 1), (1, -1), (-1, 1), (-1, -1))
DIRECTIONS = FACES_Z + FACES_Y + CORNERS


def widen(rows):
    side = jnp.zeros(rows.shape[:-1] + (C,), rows.dtype)
    return jnp.concatenate([side, rows, side], axis=-1)


def build_masks(occ_ref, mask_ref):
    row = lax.broadcasted_iota(jnp.int32, (ROWS, XC), 0) // BRICK
    for brick_z in range(ROWS // BRICK):
        mask = jnp.zeros((ROWS, XC), jnp.float32)
        for brick_y in range(ROWS // BRICK):
            flag = occ_ref[brick_z, brick_y].astype(jnp.float32)
            mask = jnp.where(row == brick_y, flag, mask)
        mask_ref[brick_z] = mask


def build_weights(w_ref, forward_ref, backward_ref):
    for ab in range(9):
        taps = w_ref[:, 192 * ab : 192 * ab + 192]
        for x in range(4):
            parts = [taps]
            if x > 0:
                parts = [jnp.zeros((C, C * x), taps.dtype)] + parts
            if x < 3:
                parts = parts + [jnp.zeros((C, C * (3 - x)), taps.dtype)]
            forward_ref[C * x : C * x + C, WINDOW * ab : WINDOW * ab + WINDOW] = (
                jnp.concatenate(parts, axis=1)
            )
        mirrored = 8 - ab
        for x in range(6):
            low = C * (x - 2)
            first, last = max(0, -low), min(192, 256 - low)
            parts = [taps[:, first:last]]
            if low > 0:
                parts = [jnp.zeros((C, low), taps.dtype)] + parts
            end = low + last
            if end < 256:
                parts = parts + [jnp.zeros((C, 256 - end), taps.dtype)]
            start = WINDOW * mirrored + C * x
            backward_ref[start : start + C, :] = jnp.concatenate(parts, axis=1)


def convolve(shifted_ref, weight_ref, transposed, mask_ref, out_ref, layers=8):
    contract = (((1,), (1 if transposed else 0,)), ((), ()))

    def block(step, _):
        first = step * layers
        mask = mask_ref[first // BRICK, :, :256]
        for quad in range(2):
            window = jnp.concatenate(
                [
                    shifted_ref[
                        b,
                        pl.ds(pl.multiple_of((first + a) * ROWS, ROWS), layers * ROWS),
                        256 * quad : 256 * quad + WINDOW,
                    ]
                    for a in range(3)
                    for b in range(3)
                ],
                axis=1,
            )
            total = lax.dot_general(
                window, weight_ref[...], contract, preferred_element_type=jnp.float32
            )
            total = total.reshape(layers, ROWS, 256) * mask[None]
            out_ref[pl.ds(first, layers), :, 256 * quad : 256 * quad + 256] = total.astype(
                jnp.bfloat16
            )
        return 0

    lax.fori_loop(0, ROWS // layers, block, 0)


def kernel_gradient(turned_ref, shifted_ref, share_ref):
    depth = ROWS + 2
    share_ref[:, TAPS * C :] = jnp.zeros((C, WIDE - TAPS * C), jnp.float32)
    for b in range(3):
        turned = jnp.concatenate(
            [
                turned_ref[:, 128 * (2 - a) : 128 * (2 - a) + 128 * depth]
                for a in range(3)
            ],
            axis=0,
        )
        window = jnp.concatenate(
            [
                shifted_ref[b, ROWS * z : ROWS * z + ROWS, 128 * p : 128 * p + 256]
                for z in range(depth)
                for p in range(4)
            ],
            axis=0,
        )
        product = jnp.dot(turned, window, preferred_element_type=jnp.float32)
        for a in range(3):
            ab = 3 * a + b
            even = product[128 * a : 128 * a + C, :192]
            odd = product[128 * a + C : 128 * a + 2 * C, C : C + 192]
            share_ref[:, 192 * ab : 192 * ab + 192] = even + odd


def mask_and_turn(raw_refs, mask_ref, padded_refs, edge_refs, turned_ref):
    turned_ref[:, :256] = jnp.zeros((128, 256), turned_ref.dtype)
    turned_ref[:, 128 * (ROWS + 2) :] = jnp.zeros((128, 256), turned_ref.dtype)

    def layer(z, _):
        mask = mask_ref[z // BRICK]
        for tensor in range(2):
            slab = raw_refs[tensor][z].astype(jnp.float32) * mask
            padded_refs[tensor][z + 1, 8:40, :] = widen(slab)
            edge_refs[tensor][0, pl.ds(z, 1), :] = slab[:1]
            edge_refs[tensor][1, pl.ds(z, 1), :] = slab[ROWS - 1 :]
            if tensor == 1:
                rows = jnp.concatenate(
                    [slab[:, 128 * p : 128 * p + 128] for p in range(4)], axis=0
                )
                column = pl.ds(pl.multiple_of(128 * (z + 2), 128), 128)
                turned_ref[:, column] = rows.T.astype(jnp.bfloat16)
        return 0

    lax.fori_loop(0, ROWS, layer, 0)


def shift_rows(padded_ref, shifted_ref):
    def layer(z, _):
        rows = pl.ds(pl.multiple_of(z * ROWS, ROWS), ROWS)
        for b in range(3):
            shifted_ref[b, rows, :] = padded_ref[z, 7 + b : 39 + b, :].astype(jnp.bfloat16)
        return 0

    lax.fori_loop(0, ROWS + 2, layer, 0)


def barrier(partners):
    semaphore = pltpu.get_barrier_semaphore()
    total = 0
    for count, partner in partners:
        total += count

        def greet(index, _, partner=partner):
            pl.semaphore_signal(
                semaphore, inc=1, device_id=partner(index), device_id_type=MESH
            )
            return 0

        lax.fori_loop(0, count, greet, 0)
    pl.semaphore_wait(semaphore, total)


def neighbour(direction):
    slabs, subs = lax.axis_size("slab"), lax.axis_size("sub")
    slab = lax.rem(lax.axis_index("slab") + direction[0] + slabs, slabs)
    sub = lax.rem(lax.axis_index("sub") + direction[1] + subs, subs)
    return slab, sub


def exchange(raw, masks, padded_refs, edge_refs, buffers, send_sem, recv_sem):
    face_send, face_recv, edge_send, edge_recv, corner_send, corner_recv = buffers
    slab, sub = lax.axis_index("slab"), lax.axis_index("sub")
    slabs, subs = lax.axis_size("slab"), lax.axis_size("sub")

    for side, (z, row) in enumerate(((ROWS, 0), (1, 1))):
        for tensor in range(2):
            face = padded_refs[tensor][z, 8:40, :]
            face_send[side, tensor] = face.astype(jnp.bfloat16)
            edge = edge_refs[tensor][1 - side]
            edge_send[side, tensor] = edge.astype(jnp.bfloat16)
    for index, (dz, dy) in enumerate(CORNERS):
        z = ROWS - 1 if dz > 0 else 0
        y = 1 if dy > 0 else 0
        corner_send[index] = jnp.concatenate(
            [edge_refs[0][y, z : z + 1, :], edge_refs[1][y, z : z + 1, :]]
            + [jnp.zeros((6, XC), jnp.float32)],
            axis=0,
        )

    copies = []
    for index, direction in enumerate(DIRECTIONS):
        if index < 2:
            source, target = face_send.at[index], face_recv.at[index]
        elif index < 4:
            source, target = edge_send.at[index - 2], edge_recv.at[index - 2]
        else:
            source, target = corner_send.at[index - 4], corner_recv.at[index - 4]
        copy = pltpu.make_async_remote_copy(
            src_ref=source,
            dst_ref=target,
            send_sem=send_sem.at[index],
            recv_sem=recv_sem.at[index],
            device_id=neighbour(direction),
            device_id_type=MESH,
        )
        copy.start()
        copies.append(copy)

    def within(direction):
        dz, dy = direction
        inside = jnp.int32(1)
        if dz:
            inside = inside * jnp.where(slab == (0 if dz > 0 else slabs - 1), 0, 1)
        if dy:
            inside = inside * jnp.where(sub == (0 if dy > 0 else subs - 1), 0, 1)
        return inside.astype(jnp.float32)

    def place():
        for copy in copies:
            copy.wait()
        for index, direction in enumerate(FACES_Z):
            layer = 0 if index == 0 else ROWS + 1
            for tensor in range(2):
                face = face_recv[index, tensor].astype(jnp.float32) * within(direction)
                padded_refs[tensor][layer, 8:40, :] = face
        for index, direction in enumerate(FACES_Y):
            row = 7 if index == 0 else 40
            for tensor in range(2):
                edge_refs[tensor][index] = edge_recv[index, tensor].astype(
                    jnp.float32
                ) * within(direction)
        for index, direction in enumerate(CORNERS):
            layer = 0 if direction[0] > 0 else ROWS + 1
            row = 7 if direction[1] > 0 else 40
            for tensor in range(2):
                corner = corner_recv[index, tensor : tensor + 1, :] * within(direction)
                padded_refs[tensor][layer, row : row + 1, :] = widen(corner)

        def layer_edges(z, _):
            for side, row in enumerate((7, 40)):
                for tensor in range(2):
                    edge = edge_refs[tensor][side, pl.ds(z, 1), :]
                    padded_refs[tensor][z + 1, row : row + 1, :] = widen(edge)
            return 0

        lax.fori_loop(0, ROWS, layer_edges, 0)

    return place


def convolution_kernel(
    features_hbm,
    cotangent_hbm,
    weight_ref,
    occ_ref,
    out_ref,
    grad_ref,
    share_ref,
    features_ref,
    cotangent_ref,
    mask_ref,
    padded_in,
    padded_grad,
    edge_in,
    edge_grad,
    shifted_in,
    shifted_grad,
    turned_ref,
    forward_ref,
    backward_ref,
    face_send,
    face_recv,
    edge_send,
    edge_recv,
    corner_send,
    corner_recv,
    load_sem,
    send_sem,
    recv_sem,
):
    loads = [
        pltpu.make_async_copy(features_hbm, features_ref, load_sem.at[0]),
        pltpu.make_async_copy(cotangent_hbm, cotangent_ref, load_sem.at[1]),
    ]
    for load in loads:
        load.start()
    semaphore = pltpu.get_barrier_semaphore()
    for direction in DIRECTIONS:
        pl.semaphore_signal(
            semaphore, inc=1, device_id=neighbour(direction), device_id_type=MESH
        )
    build_masks(occ_ref, mask_ref)
    for load in loads:
        load.wait()
    padded_refs, edge_refs = (padded_in, padded_grad), (edge_in, edge_grad)
    mask_and_turn(
        (features_ref, cotangent_ref), mask_ref, padded_refs, edge_refs, turned_ref
    )
    pl.semaphore_wait(semaphore, len(DIRECTIONS))
    buffers = (face_send, face_recv, edge_send, edge_recv, corner_send, corner_recv)
    place = exchange(
        (features_ref, cotangent_ref), mask_ref, padded_refs, edge_refs, buffers, send_sem, recv_sem
    )
    build_weights(weight_ref, forward_ref, backward_ref)
    place()
    shift_rows(padded_in, shifted_in)
    kernel_gradient(turned_ref, shifted_in, share_ref)
    shift_rows(padded_grad, shifted_grad)
    convolve(shifted_in, forward_ref, True, mask_ref, out_ref)
    convolve(shifted_grad, backward_ref, False, mask_ref, grad_ref)


def convolution_scratch():
    bf16, f32 = jnp.bfloat16, jnp.float32
    return [
        pltpu.VMEM((ROWS, ROWS, XC), bf16),
        pltpu.VMEM((ROWS, ROWS, XC), bf16),
        pltpu.VMEM((ROWS // BRICK, ROWS, XC), f32),
        pltpu.VMEM((ROWS + 2, 48, PADX), f32),
        pltpu.VMEM((ROWS + 2, 48, PADX), f32),
        pltpu.VMEM((2, ROWS, XC), f32),
        pltpu.VMEM((2, ROWS, XC), f32),
        pltpu.VMEM((3, (ROWS + 2) * ROWS, PADX), bf16),
        pltpu.VMEM((3, (ROWS + 2) * ROWS, PADX), bf16),
        pltpu.VMEM((128, 128 * (ROWS + 4)), bf16),
        pltpu.VMEM((256, 9 * WINDOW), bf16),
        pltpu.VMEM((9 * WINDOW, 256), bf16),
        pltpu.VMEM((2, 2, ROWS, PADX), bf16),
        pltpu.VMEM((2, 2, ROWS, PADX), bf16),
        pltpu.VMEM((2, 2, ROWS, XC), bf16),
        pltpu.VMEM((2, 2, ROWS, XC), bf16),
        pltpu.VMEM((4, 8, XC), f32),
        pltpu.VMEM((4, 8, XC), f32),
        pltpu.SemaphoreType.DMA((2,)),
        pltpu.SemaphoreType.DMA((8,)),
        pltpu.SemaphoreType.DMA((8,)),
    ]


def plane_partner(index):
    slab, sub = lax.axis_index("slab"), lax.axis_index("sub")
    place = lax.rem(lax.rem(slab, 8) * 4 + sub + index + 1, PLANE)
    return (slab // 8 * 8 + place // 4, lax.rem(place, 4)), place


def column_partner(index):
    slab, sub = lax.axis_index("slab"), lax.axis_index("sub")
    z = lax.rem(slab // 8 + index + 1, lax.axis_size("slab") // 8)
    return (z * 8 + lax.rem(slab, 8), sub), z


def half_partner(index):
    slab, sub = lax.axis_index("slab"), lax.axis_index("sub")
    z = slab // 8
    z = z // PIECES * PIECES + lax.rem(z + index + 1, PIECES)
    return (z * 8 + lax.rem(slab, 8), sub), z


def chunk(ref, place):
    row = pl.multiple_of(place // 4 * 8, 8)
    lane = pl.multiple_of(lax.rem(place, 4) * CHUNK, CHUNK)
    return ref.at[pl.ds(row, 8), pl.ds(lane, CHUNK)]


def spread(count, copy):
    def start(index, _):
        copy(index).start()
        return 0

    lax.fori_loop(0, count, start, 0)


def settle(count, copy):
    def wait(index, _):
        copy(index).wait()
        return 0

    lax.fori_loop(0, count, wait, 0)


def sum_kernel(
    share_ref,
    result_ref,
    plane_recv,
    rows_ref,
    column_recv,
    done_ref,
    full_ref,
    plane_send_sem,
    plane_recv_sem,
    column_send_sem,
    column_recv_sem,
    half_send_sem,
    half_recv_sem,
    gather_send_sem,
    gather_recv_sem,
):
    deep = lax.axis_size("slab") // 8
    slab, sub = lax.axis_index("slab"), lax.axis_index("sub")
    z, place = slab // 8, lax.rem(slab, 8) * 4 + sub
    barrier(
        [
            (PLANE - 1, lambda index: plane_partner(index)[0]),
            (deep - 1, lambda index: column_partner(index)[0]),
        ]
    )

    def to_plane(index):
        device, other = plane_partner(index)
        return pltpu.make_async_remote_copy(
            src_ref=chunk(share_ref, other),
            dst_ref=plane_recv.at[index],
            send_sem=plane_send_sem.at[index],
            recv_sem=plane_recv_sem.at[index],
            device_id=device,
            device_id_type=MESH,
        )

    def to_column(index):
        device, other = column_partner(index)
        return pltpu.make_async_remote_copy(
            src_ref=rows_ref.at[lax.rem(other, PIECES)],
            dst_ref=column_recv.at[index],
            send_sem=column_send_sem.at[index],
            recv_sem=column_recv_sem.at[index],
            device_id=device,
            device_id_type=MESH,
        )

    own = lax.rem(z, PIECES)

    def to_half(index):
        device, _ = half_partner(index)
        return pltpu.make_async_remote_copy(
            src_ref=done_ref.at[own],
            dst_ref=done_ref.at[own],
            send_sem=half_send_sem.at[index],
            recv_sem=half_recv_sem.at[index],
            device_id=device,
            device_id_type=MESH,
        )

    def to_all(index):
        device, _ = plane_partner(index)
        return pltpu.make_async_remote_copy(
            src_ref=chunk(full_ref, place),
            dst_ref=chunk(full_ref, place),
            send_sem=gather_send_sem.at[index],
            recv_sem=gather_recv_sem.at[index],
            device_id=device,
            device_id_type=MESH,
        )

    spread(PLANE - 1, to_plane)
    settle(PLANE - 1, to_plane)
    total = chunk(share_ref, place)[...]
    for index in range(PLANE - 1):
        total = total + plane_recv[index]
    for row in range(PIECES):
        rows_ref[row] = total[row : row + 1]
    spread(deep - 1, to_column)
    settle(deep - 1, to_column)
    piece = rows_ref[own]
    for index in range(deep - 1):
        piece = piece + column_recv[index]
    done_ref[own] = piece
    spread(PIECES - 1, to_half)
    settle(PIECES - 1, to_half)
    mine = chunk(full_ref, place)
    mine[...] = jnp.concatenate([done_ref[row] for row in range(PIECES)], axis=0)
    spread(PLANE - 1, to_all)
    settle(PLANE - 1, to_all)
    cells = lax.axis_size("slab") * lax.axis_size("sub") * ROWS * ROWS * BRICK
    result_ref[...] = full_ref[:, : TAPS * C] * cells ** (-0.5)


def sum_scratch(deep):
    f32, dma = jnp.float32, pltpu.SemaphoreType.DMA
    return [
        pltpu.VMEM((PLANE - 1, 8, CHUNK), f32),
        pltpu.VMEM((PIECES, 1, CHUNK), f32),
        pltpu.VMEM((deep - 1, 1, CHUNK), f32),
        pltpu.VMEM((PIECES, 1, CHUNK), f32),
        pltpu.VMEM((C, WIDE), f32),
        dma((PLANE - 1,)),
        dma((PLANE - 1,)),
        dma((deep - 1,)),
        dma((deep - 1,)),
        dma((PIECES - 1,)),
        dma((PIECES - 1,)),
        dma((PLANE - 1,)),
        dma((PLANE - 1,)),
    ]


def convolutions(features, cotangent, weight, occupancy):
    vmem, hbm = pl.BlockSpec(memory_space=pltpu.VMEM), pl.BlockSpec(memory_space=pl.ANY)
    return pl.pallas_call(
        convolution_kernel,
        out_shape=[
            jax.ShapeDtypeStruct(features.shape, jnp.bfloat16),
            jax.ShapeDtypeStruct(features.shape, jnp.bfloat16),
            jax.ShapeDtypeStruct((C, WIDE), jnp.float32),
        ],
        in_specs=[hbm, hbm, vmem, pl.BlockSpec(memory_space=pltpu.SMEM)],
        out_specs=[vmem, vmem, vmem],
        scratch_shapes=convolution_scratch(),
        compiler_params=pltpu.CompilerParams(
            collective_id=0, has_side_effects=True, vmem_limit_bytes=56 * 2**20
        ),
        cost_estimate=pl.CostEstimate(
            flops=11 * 10**9, bytes_accessed=5 * 2**20, transcendentals=0
        ),
        name="convolutions",
    )(features, cotangent, weight, occupancy)


def sum_shares(share, deep):
    vmem = pl.BlockSpec(memory_space=pltpu.VMEM)
    return pl.pallas_call(
        sum_kernel,
        out_shape=jax.ShapeDtypeStruct((C, TAPS * C), jnp.float32),
        in_specs=[vmem],
        out_specs=vmem,
        scratch_shapes=sum_scratch(deep),
        compiler_params=pltpu.CompilerParams(
            collective_id=1, has_side_effects=True, vmem_limit_bytes=16 * 2**20
        ),
        cost_estimate=pl.CostEstimate(
            flops=10**7, bytes_accessed=2 * 2**20, transcendentals=0
        ),
        name="sum_shares",
    )(share)


def per_device(features, cotangent, weight, occupancy):
    out, grad, share = convolutions(features, cotangent, weight, occupancy)
    total = sum_shares(share, lax.axis_size("slab") // 8)
    return out, grad, total


def solution(mesh):
    placed = (P("slab", "sub", None), P("slab", "sub", None), P(), P("slab", "sub"))
    return jax.shard_map(
        per_device,
        mesh=mesh,
        in_specs=placed,
        out_specs=(P("slab", "sub", None), P("slab", "sub", None), P()),
        check_vma=False,
    )
```

time: 1070 us -> 85.2 us (0.08); the launches traced: 1060 us -> 85 us
  waiting for transfers between devices: 738 us -> 0 us
  local copies, waits for them, and re-layouts: 240 us -> 5.17 us
  Pallas kernels: 0 us -> 79.1 us
  matrix products: 33.2 us -> 0 us
  starting transfers between devices: 13.7 us -> 0 us
  between operations: 14.3 us -> 0.66 us
  other arithmetic: 12.7 us -> 0 us
    psum x1 -> x0, waiting for transfers between devices: 734 us -> none  [per_device(): weight_grad = lax.psum(weight_sum, ('slab', 'sub')) * total_cells ** (-0.5)]
    slice x56 -> x0, local copies, waits for them, and re-layouts: 83.1 us -> none  [the longest x24 29.1 us: tap_columns(): grid_cells[shift_z:shift_z + BRICK, shift_y:shift_y + BRICK, shift_x:shif...]
    pallas_call x0 -> x2, Pallas kernels: none -> 79.1 us  [the longest x1 41.1 us: sum_shares(): pl.pallas_call(sum_kernel, out_shape=jax.ShapeDtypeStruct((C, TAPS * C),...]
    concatenate x13 -> x0, local copies, waits for them, and re-layouts: 57.6 us -> none  [the longest x12 55.1 us: tap_columns(): return jnp.concatenate(columns, axis=1)]
    another operation x18 -> x0, local copies, waits for them, and re-layouts: 42 us -> none  [the longest x17 41.9 us: per_device(): brick_items = jnp.stack(pieces)]
    dot_general x20 -> x0, matrix products: 33.2 us -> none  [the longest x6 13.5 us: brick_terms(): jnp.dot(grad_cols, weight_back, preferred_element_type=jnp.float32)]
    dynamic_slice x6 -> x0, local copies, waits for them, and re-layouts: 18.9 us -> none  [advance(): lax.dynamic_index_in_dim(brick_items, item_index, 0, keepdims=False)]
    reshape x10 -> x0, local copies, waits for them, and re-layouts: 18.1 us -> none  [the longest x1 6.4 us: per_device(): slot_out.reshape(BZ, BY, 2, BRICK, BRICK, BRICK, C)]
  transfers between devices with their start and end apart: 5 -> 0, of which waited for: 3 -> 0; matrix products, arithmetic and copies ran while one was open for 1% -> 0% of each run, Pallas kernels for 0% -> 0%
where the time goes in v1:
time: 85.2 us; the launch traced here: 85 us
  Pallas kernels  79.1 us (93%)
  local copies, waits for them, and re-layouts  5.17 us (6%)
    pallas_call x1, Pallas kernels, sum_shares(): pl.pallas_call(sum_kernel, out_shape=jax.ShapeDtypeStruct((C, TAPS * C),...  41.1 us
    pallas_call x1, Pallas kernels, convolutions(): pl.pallas_call(convolution_kernel, out_shape=[jax.ShapeDtypeStruct(featur...  38 us
    unnamed x7, local copies, waits for them, and re-layouts  5.17 us

profile of v1, /device:TPU:1, one launch (start us, length us, event | category | flops | bytes accessed | tf_op | source)
XLA Modules:
  0.0 85.0 jit_solution(8203263062447965577)
XLA Ops:
  0.6 38.0 %convolutions.1 = (bf16[32,32,512]{2,1,0:T(8,128)(2,1)}, bf16[32,32,512]{2,1,0:T(8,128)(2,1)}, f32[64,2048]{1,0:T(8,128)}) custom-call(bf16[32,32,512]{2,1,0:T(8,128)(2,1)} %features_hbm.1, bf16[32,32,512]{2,1,0:T(8,128)(2,1)} %cotangent_hbm.1, bf16[64,1728]{1,0:T(8,128)(2,1)} %weight_ref.1, s32[4,4]{1,0:T(4,128)} %occ_ref.1), custom_call_target="tpu_custom_call" | custom-call | flops 11000000512 | bytes 5242880 | tf_op jit(solution)/shard_map/convolutions/pallas_call | solution.py:511
  38.6 0.0 copy-start
  38.6 1.0 %copy-done = f32[64,2048]{1,0:T(8,128)S(1)} copy-done((f32[64,2048]{1,0:T(8,128)S(1)}, f32[64,2048]{1,0:T(8,128)}, u32[]{:S(2)}) %copy-start) | copy-done | bytes 524312
  39.7 41.1 %sum_shares.1 = f32[64,1728]{1,0:T(8,128)S(1)} custom-call(f32[64,2048]{1,0:T(8,128)S(1)} %copy-done), custom_call_target="tpu_custom_call" | custom-call | flops 10000000 | bytes 2097152 | tf_op jit(solution)/shard_map/sum_shares/pallas_call | solution.py:533
  80.8 0.0 copy-start.1
  80.8 2.4 %copy.10 = bf16[32,32,512]{2,1,0:T(8,128)(2,1)} copy(bf16[32,32,512]{2,1,0:T(8,128)(2,1)} %get-tuple-element.12) | data formatting | bytes 2097152
  83.2 0.0 copy-done.1
  83.2 1.0 %copy.11 = bf16[32,32,512]{2,1,0:T(8,128)(2,1)} copy(bf16[32,32,512]{2,1,0:T(8,128)(2,1)S(1)} %copy-done.1) | data formatting | bytes 2097152
  84.2 0.8 copy.12
Async XLA Ops:
  38.6 1.0 %copy-start = (f32[64,2048]{1,0:T(8,128)S(1)}, f32[64,2048]{1,0:T(8,128)}, u32[]{:S(2)}) copy-start(f32[64,2048]{1,0:T(8,128)} %get-tuple-element.8.share_ref) | copy-start | bytes 1572868
  80.8 2.4 %copy-start.1 = (bf16[32,32,512]{2,1,0:T(8,128)(2,1)S(1)}, bf16[32,32,512]{2,1,0:T(8,128)(2,1)}, u32[]{:S(2)}) copy-start(bf16[32,32,512]{2,1,0:T(8,128)(2,1)} %get-tuple-element.13) | copy-start | bytes 3145732

commit v2 on v0

v2 whole, which is shorter than its diff:
```python
import jax
import jax.numpy as jnp
from jax import lax
from jax.experimental import pallas as pl
from jax.experimental.pallas import tpu as pltpu
from jax.sharding import PartitionSpec as P

C = 64
BRICK = 8
ROWS = 32
XC = 512
PADX = XC + 2 * C
WINDOW = 384
TAPS = 27
MESH = pl.DeviceIdType.MESH
DEEP = 16
PLANE = 16
PIECES = 4
CHUNK = 512
WIDE = 4 * CHUNK
HALF = C // 2

FACES_Z = ((1, 0), (-1, 0))
FACES_Y = ((0, 1), (0, -1))
CORNERS = ((1, 1), (1, -1), (-1, 1), (-1, -1))
DIRECTIONS = FACES_Z + FACES_Y + CORNERS


def widen(rows):
    side = jnp.zeros(rows.shape[:-1] + (C,), rows.dtype)
    return jnp.concatenate([side, rows, side], axis=-1)


def pairs(rows):
    return jnp.concatenate([rows[:, 128 * p : 128 * p + 128] for p in range(4)], axis=0)


def pair_windows(rows):
    return jnp.concatenate([rows[:, 128 * p : 128 * p + 256] for p in range(4)], axis=0)


def build_masks(occ_ref, mask_ref, narrow_ref):
    row = lax.broadcasted_iota(jnp.int32, (ROWS, XC), 0) // BRICK
    for brick_z in range(ROWS // BRICK):
        mask = jnp.zeros((ROWS, XC), jnp.float32)
        for brick_y in range(ROWS // BRICK):
            flag = occ_ref[brick_z, brick_y].astype(jnp.float32)
            mask = jnp.where(row == brick_y, flag, mask)
        mask_ref[brick_z] = mask
        narrow_ref[brick_z] = mask.astype(jnp.bfloat16)


def build_weights(w_ref, forward_ref, backward_ref):
    for ab in range(9):
        taps = w_ref[:, 192 * ab : 192 * ab + 192]
        for x in range(4):
            parts = [taps]
            if x > 0:
                parts = [jnp.zeros((C, C * x), taps.dtype)] + parts
            if x < 3:
                parts = parts + [jnp.zeros((C, C * (3 - x)), taps.dtype)]
            forward_ref[C * x : C * x + C, WINDOW * ab : WINDOW * ab + WINDOW] = (
                jnp.concatenate(parts, axis=1)
            )
        mirrored = 8 - ab
        for x in range(6):
            low = C * (x - 2)
            first, last = max(0, -low), min(192, 256 - low)
            parts = [taps[:, first:last]]
            if low > 0:
                parts = [jnp.zeros((C, low), taps.dtype)] + parts
            end = low + last
            if end < 256:
                parts = parts + [jnp.zeros((C, 256 - end), taps.dtype)]
            start = WINDOW * mirrored + C * x
            backward_ref[start : start + C, :] = jnp.concatenate(parts, axis=1)


def clear_sides(stage_ref, turned_ref, share_ref):
    for side in range(2):
        stage_ref[side, 0:8, :] = jnp.zeros((8, PADX), jnp.float32)
        stage_ref[side, 40:48, :] = jnp.zeros((8, PADX), jnp.float32)
    for b in range(3):
        turned_ref[b, :, :128] = jnp.zeros((128, 128), turned_ref.dtype)
        turned_ref[b, :, 128 * (ROWS + 1) :] = jnp.zeros((128, 128), turned_ref.dtype)
    share_ref[:, TAPS * C :] = jnp.zeros((C, WIDE - TAPS * C), jnp.float32)


def cut_faces(raw_refs, mask_ref, edge_refs, buffers):
    face_send, _, edge_send, _, corner_send, _ = buffers

    def layer(z, _):
        mask = mask_ref[z // BRICK]
        for tensor in range(2):
            for side, tile in enumerate((0, ROWS - 16)):
                rows = raw_refs[tensor][z, tile : tile + 16, :].astype(jnp.float32)
                row = 0 if side == 0 else 15
                edge_refs[tensor][side, pl.ds(z, 1), :] = (
                    rows[row : row + 1] * mask[tile + row : tile + row + 1]
                )
        return 0

    lax.fori_loop(0, ROWS, layer, 0, unroll=4)
    for side, z in enumerate((ROWS - 1, 0)):
        for tensor in range(2):
            face = raw_refs[tensor][z].astype(jnp.float32) * mask_ref[z // BRICK]
            face_send[side, tensor] = face.astype(jnp.bfloat16)
            edge_send[side, tensor] = edge_refs[tensor][1 - side].astype(jnp.bfloat16)
    for index, (dz, dy) in enumerate(CORNERS):
        z = ROWS - 1 if dz > 0 else 0
        y = 1 if dy > 0 else 0
        corner_send[index] = jnp.concatenate(
            [edge_refs[0][y, z : z + 1, :], edge_refs[1][y, z : z + 1, :]]
            + [jnp.zeros((6, XC), jnp.float32)],
            axis=0,
        )


def prepare(raw_ref, narrow_ref, shifted_ref, unroll=8):
    def layer(z, _):
        rows = pl.ds(pl.multiple_of((z + 1) * ROWS, ROWS), ROWS)
        shifted_ref[1, rows, :] = widen(raw_ref[z] * narrow_ref[z // BRICK])
        return 0

    lax.fori_loop(0, ROWS, layer, 0, unroll=unroll)


def prepare_both(features_ref, cotangent_ref, narrow_ref, shifted_ref, turned_ref):
    edge = jnp.zeros((128, 1), jnp.bfloat16)
    row = lax.broadcasted_iota(jnp.int32, (128, 128), 1) % ROWS
    not_last = (row != ROWS - 1).astype(jnp.float32).astype(jnp.bfloat16)
    not_first = (row != 0).astype(jnp.float32).astype(jnp.bfloat16)

    def layer(z, _):
        mask = narrow_ref[z // BRICK]
        rows = pl.ds(pl.multiple_of((z + 1) * ROWS, ROWS), ROWS)
        shifted_ref[1, rows, :] = widen(features_ref[z] * mask)
        column = pl.ds(pl.multiple_of(128 * (z + 1), 128), 128)
        turned = pairs(cotangent_ref[z] * mask).T
        turned_ref[0, :, column] = not_last * jnp.concatenate([turned[:, 1:], edge], axis=1)
        turned_ref[1, :, column] = turned
        turned_ref[2, :, column] = not_first * jnp.concatenate([edge, turned[:, :127]], axis=1)
        return 0

    lax.fori_loop(0, ROWS, layer, 0, unroll=8)


def pad_rows(shifted_ref, padded_ref):
    def layer(z, _):
        rows = pl.ds(pl.multiple_of((z + 1) * ROWS, ROWS), ROWS)
        padded_ref[z + 1, 8:40, :] = shifted_ref[1, rows, :].astype(jnp.float32)
        return 0

    lax.fori_loop(0, ROWS, layer, 0, unroll=4)


def shift_layer(padded_ref, shifted_ref, z, shifts):
    rows = pl.ds(pl.multiple_of(z * ROWS, ROWS), ROWS)
    for b in shifts:
        shifted_ref[b, rows, :] = padded_ref[z, 7 + b : 39 + b, :].astype(jnp.bfloat16)


def shift_rows(padded_ref, shifted_ref):
    def layer(z, _):
        shift_layer(padded_ref, shifted_ref, z, (0, 2))
        return 0

    lax.fori_loop(1, ROWS + 1, layer, 0, unroll=8)


def inner_gradient(turned_ref, shifted_ref, product_ref):
    window = jnp.concatenate(
        [
            shifted_ref[1, ROWS * z : ROWS * z + ROWS, 128 * p : 128 * p + 256]
            for z in range(1, ROWS + 1)
            for p in range(4)
        ],
        axis=0,
    )
    for b in range(3):
        turned = jnp.concatenate(
            [turned_ref[b, :, 128 * (2 - a) : 128 * (2 - a + ROWS)] for a in range(3)],
            axis=0,
        )
        product_ref[b] = jnp.dot(turned, window, preferred_element_type=jnp.float32)


def outer_gradient(turned_ref, shifted_ref, edge_turned_ref, stage_ref, product_ref, share_ref):
    def along_z(z, layer):
        first = ROWS * layer
        window = jnp.concatenate(
            [pair_windows(shifted_ref[b, first : first + ROWS, :]) for b in range(3)],
            axis=1,
        )
        column = turned_ref[1, :, 128 * (z + 1) : 128 * (z + 2)]
        return jnp.dot(column, window, preferred_element_type=jnp.float32)

    def along_y(side):
        window = jnp.concatenate(
            [
                pair_windows(stage_ref[side, 7 + a : 39 + a, :].astype(jnp.bfloat16))
                for a in range(3)
            ],
            axis=1,
        )
        return jnp.dot(edge_turned_ref[side], window, preferred_element_type=jnp.float32)

    low_z, high_z = along_z(0, 0), along_z(ROWS - 1, ROWS + 1)
    edges = {0: along_y(0), 2: along_y(1)}
    for b in range(3):
        for a in range(3):
            term = product_ref[b, 128 * a : 128 * a + 128, :]
            if a == 0:
                term = term + low_z[:, 256 * b : 256 * b + 256]
            if a == 2:
                term = term + high_z[:, 256 * b : 256 * b + 256]
            if b != 1:
                term = term + edges[b][:, 256 * a : 256 * a + 256]
            ab = 3 * a + b
            share_ref[:, 192 * ab : 192 * ab + 192] = (
                term[:C, :192] + term[C:, C : C + 192]
            )


def convolve(shifted_ref, weight_ref, transposed, mask_ref, out_ref, start, stop, layers=BRICK):
    contract = (((1,), (1 if transposed else 0,)), ((), ()))

    def block(step, _):
        first = step * layers
        mask = mask_ref[first // BRICK, :, :256]
        for quad in range(2):
            window = jnp.concatenate(
                [
                    shifted_ref[
                        b,
                        pl.ds(pl.multiple_of((first + a) * ROWS, ROWS), layers * ROWS),
                        256 * quad : 256 * quad + WINDOW,
                    ]
                    for a in range(3)
                    for b in range(3)
                ],
                axis=1,
            )
            total = lax.dot_general(
                window, weight_ref[...], contract, preferred_element_type=jnp.float32
            )
            total = total.reshape(layers, ROWS, 256) * mask[None]
            out_ref[pl.ds(first, layers), :, 256 * quad : 256 * quad + 256] = total.astype(
                jnp.bfloat16
            )
        return 0

    lax.fori_loop(start, stop, block, 0)


def neighbour(direction):
    slabs, subs = lax.axis_size("slab"), lax.axis_size("sub")
    slab = lax.rem(lax.axis_index("slab") + direction[0] + slabs, slabs)
    sub = lax.rem(lax.axis_index("sub") + direction[1] + subs, subs)
    return slab, sub


def within(direction):
    dz, dy = direction
    inside = jnp.int32(1)
    if dz:
        edge = 0 if dz > 0 else lax.axis_size("slab") - 1
        inside = inside * jnp.where(lax.axis_index("slab") == edge, 0, 1)
    if dy:
        edge = 0 if dy > 0 else lax.axis_size("sub") - 1
        inside = inside * jnp.where(lax.axis_index("sub") == edge, 0, 1)
    return inside.astype(jnp.float32)


def halo_copies(buffers, send_sem, recv_sem):
    face_send, face_recv, edge_send, edge_recv, corner_send, corner_recv = buffers
    copies = []
    for index, direction in enumerate(DIRECTIONS):
        if index < 2:
            source, target = face_send.at[index], face_recv.at[index]
        elif index < 4:
            source, target = edge_send.at[index - 2], edge_recv.at[index - 2]
        else:
            source, target = corner_send.at[index - 4], corner_recv.at[index - 4]
        copies.append(
            pltpu.make_async_remote_copy(
                src_ref=source,
                dst_ref=target,
                send_sem=send_sem.at[index],
                recv_sem=recv_sem.at[index],
                device_id=neighbour(direction),
                device_id_type=MESH,
            )
        )
    return copies


def place_layers(tensor, buffers, padded_ref):
    _, face_recv, _, _, _, corner_recv = buffers
    for index, direction in enumerate(FACES_Z):
        layer = 0 if index == 0 else ROWS + 1
        face = face_recv[index, tensor].astype(jnp.float32) * within(direction)
        padded_ref[layer, 8:40, :] = widen(face)
    for index, direction in enumerate(CORNERS):
        layer = 0 if direction[0] > 0 else ROWS + 1
        row = 7 if direction[1] > 0 else 40
        corner = corner_recv[index, tensor : tensor + 1, :] * within(direction)
        padded_ref[layer, row : row + 1, :] = widen(corner)


def stage_edges(tensor, buffers, stage_ref):
    _, _, _, edge_recv, _, _ = buffers
    for index, direction in enumerate(FACES_Y):
        edge = edge_recv[index, tensor].astype(jnp.float32) * within(direction)
        stage_ref[index, 8:40, :] = widen(edge)


def place_rows(stage_ref, padded_ref):
    def layer(z, _):
        for side, row in enumerate((7, 40)):
            padded_ref[z + 1, row : row + 1, :] = stage_ref[side, pl.ds(8 + z, 1), :]
        return 0

    lax.fori_loop(0, ROWS, layer, 0)


def spread(count, copy):
    def start(index, _):
        copy(index).start()
        return 0

    lax.fori_loop(0, count, start, 0)


def settle(count, copy):
    def wait(index, _):
        copy(index).wait()
        return 0

    lax.fori_loop(0, count, wait, 0)


def sibling():
    slab = lax.axis_index("slab")
    return slab + 1 - 2 * lax.rem(slab, 2), lax.axis_index("sub")


def plane_place():
    return lax.rem(lax.axis_index("slab") // 2, 4) * 4 + lax.axis_index("sub")


def plane_partner(index):
    slab = lax.axis_index("slab")
    place = lax.rem(plane_place() + index + 1, PLANE)
    return (slab // 8 * 8 + place // 4 * 2 + lax.rem(slab, 2), lax.rem(place, 4)), place


def column_partner(step):
    slab = lax.axis_index("slab")
    z = lax.rem(slab // 8 + step + DEEP, DEEP)
    return (z * 8 + lax.rem(slab, 8), lax.axis_index("sub")), z


def chunk(ref, place):
    row = pl.multiple_of(place // 4 * 8, 8)
    lane = pl.multiple_of(lax.rem(place, 4) * CHUNK, CHUNK)
    return ref.at[pl.ds(row, 8), pl.ds(lane, CHUNK)]


def half(ref, core):
    return ref.at[pl.ds(pl.multiple_of(core * HALF, HALF), HALF)]


def greet():
    semaphore = pltpu.get_barrier_semaphore()

    def signal(device):
        pl.semaphore_signal(semaphore, inc=1, device_id=device, device_id_type=MESH)

    def plane(index, _):
        signal(plane_partner(index)[0])
        return 0

    def column(index, _):
        signal(column_partner(index + 1)[0])
        return 0

    for direction in DIRECTIONS:
        signal(neighbour(direction))
    signal(sibling())
    lax.fori_loop(0, PLANE - 1, plane, 0)
    lax.fori_loop(0, DEEP - 1, column, 0)
    return lambda: pl.semaphore_wait(
        semaphore, len(DIRECTIONS) + 1 + (PLANE - 1) + (DEEP - 1)
    )


def kernel(
    features_hbm,
    cotangent_hbm,
    weight_hbm,
    occ_hbm,
    out_ref,
    grad_ref,
    result_ref,
    features_ref,
    cotangent_ref,
    weight_ref,
    occ_ref,
    mask_ref,
    narrow_ref,
    padded_in,
    padded_grad,
    edge_in,
    edge_grad,
    stage_ref,
    shifted_in,
    shifted_grad,
    turned_ref,
    edge_turned_ref,
    forward_ref,
    backward_ref,
    product_ref,
    share_ref,
    face_send,
    face_recv,
    edge_send,
    edge_recv,
    corner_send,
    corner_recv,
    core_recv,
    half_ref,
    plane_recv,
    pieces_ref,
    column_recv,
    done_ref,
    full_ref,
    load_sem,
    halo_send_sem,
    halo_recv_sem,
    core_sem,
    plane_send_sem,
    plane_recv_sem,
    column_send_sem,
    column_recv_sem,
    near_send_sem,
    near_recv_sem,
    gather_send_sem,
    gather_recv_sem,
):
    loads = [
        pltpu.make_async_copy(features_hbm, features_ref, load_sem.at[0]),
        pltpu.make_async_copy(cotangent_hbm, cotangent_ref, load_sem.at[1]),
        pltpu.make_async_copy(weight_hbm, weight_ref, load_sem.at[2]),
    ]
    flags = pltpu.make_async_copy(occ_hbm, occ_ref, load_sem.at[3])
    slab = lax.axis_index("slab")
    z, core, place = slab // 8, lax.rem(slab, 2), plane_place()
    own = lax.rem(z, PIECES)
    buffers = (face_send, face_recv, edge_send, edge_recv, corner_send, corner_recv)
    halos = halo_copies(buffers, halo_send_sem, halo_recv_sem)
    to_sibling = pltpu.make_async_remote_copy(
        src_ref=half(share_ref, 1 - core),
        dst_ref=core_recv,
        send_sem=core_sem.at[0],
        recv_sem=core_sem.at[1],
        device_id=sibling(),
        device_id_type=MESH,
    )

    def to_plane(index):
        device, other = plane_partner(index)
        return pltpu.make_async_remote_copy(
            src_ref=chunk(half_ref, other),
            dst_ref=plane_recv.at[index],
            send_sem=plane_send_sem.at[index],
            recv_sem=plane_recv_sem.at[index],
            device_id=device,
            device_id_type=MESH,
        )

    def to_column(index):
        device, other = column_partner(index + 1)
        return pltpu.make_async_remote_copy(
            src_ref=pieces_ref.at[lax.rem(other, PIECES)],
            dst_ref=column_recv.at[z],
            send_sem=column_send_sem.at[index],
            recv_sem=column_recv_sem.at[index],
            device_id=device,
            device_id_type=MESH,
        )

    def to_near(index):
        device, _ = column_partner((-1, 1, -2)[index])
        return pltpu.make_async_remote_copy(
            src_ref=done_ref.at[own],
            dst_ref=done_ref.at[own],
            send_sem=near_send_sem.at[index],
            recv_sem=near_recv_sem.at[index],
            device_id=device,
            device_id_type=MESH,
        )

    def to_all(index):
        device, _ = plane_partner(index)
        mine = chunk(half(full_ref, core), place)
        return pltpu.make_async_remote_copy(
            src_ref=mine,
            dst_ref=mine,
            send_sem=gather_send_sem.at[index],
            recv_sem=gather_recv_sem.at[index],
            device_id=device,
            device_id_type=MESH,
        )

    back_to_sibling = pltpu.make_async_remote_copy(
        src_ref=half(full_ref, core),
        dst_ref=half(full_ref, core),
        send_sem=core_sem.at[2],
        recv_sem=core_sem.at[3],
        device_id=sibling(),
        device_id_type=MESH,
    )

    flags.start()
    for load in loads:
        load.start()
    everyone_here = greet()
    clear_sides(stage_ref, turned_ref, share_ref)
    flags.wait()
    build_masks(occ_ref, mask_ref, narrow_ref)
    for load in loads:
        load.wait()
    cut_faces((features_ref, cotangent_ref), mask_ref, (edge_in, edge_grad), buffers)
    everyone_here()
    for copy in halos:
        copy.start()

    prepare_both(features_ref, cotangent_ref, narrow_ref, shifted_in, turned_ref)
    for side in range(2):
        edge_turned_ref[side] = pairs(edge_grad[side]).T.astype(jnp.bfloat16)
    inner_gradient(turned_ref, shifted_in, product_ref)

    for copy in halos:
        copy.wait()
    place_layers(0, buffers, padded_in)
    for layer in (0, ROWS + 1):
        shift_layer(padded_in, shifted_in, layer, (0, 1, 2))
    stage_edges(0, buffers, stage_ref)
    outer_gradient(
        turned_ref, shifted_in, edge_turned_ref, stage_ref, product_ref, share_ref
    )
    to_sibling.start()

    build_weights(weight_ref, forward_ref, backward_ref)
    pad_rows(shifted_in, padded_in)
    to_sibling.wait()
    half_ref[...] = half(share_ref, core)[...] + core_recv[...]
    spread(PLANE - 1, to_plane)

    place_rows(stage_ref, padded_in)
    shift_rows(padded_in, shifted_in)
    convolve(shifted_in, forward_ref, True, mask_ref, out_ref, 0, 3)
    settle(PLANE - 1, to_plane)
    total = chunk(half_ref, place)[...]
    for index in range(PLANE - 1):
        total = total + plane_recv[index]
    for piece in range(PIECES):
        pieces_ref[piece] = total[:, 128 * piece : 128 * piece + 128]
    spread(DEEP - 1, to_column)

    convolve(shifted_in, forward_ref, True, mask_ref, out_ref, 3, 4)
    prepare(cotangent_ref, narrow_ref, shifted_grad)
    pad_rows(shifted_grad, padded_grad)
    place_layers(1, buffers, padded_grad)
    stage_edges(1, buffers, stage_ref)
    place_rows(stage_ref, padded_grad)
    shift_rows(padded_grad, shifted_grad)
    for layer in (0, ROWS + 1):
        shift_layer(padded_grad, shifted_grad, layer, (0, 1, 2))
    convolve(shifted_grad, backward_ref, False, mask_ref, grad_ref, 0, 2)
    settle(DEEP - 1, to_column)
    column_recv[z] = pieces_ref[own]
    piece = column_recv[0]
    for index in range(1, DEEP):
        piece = piece + column_recv[index]
    done_ref[own] = piece
    for index in range(PIECES - 1):
        to_near(index).start()

    convolve(shifted_grad, backward_ref, False, mask_ref, grad_ref, 2, 4)
    for index in range(PIECES - 1):
        to_near(index).wait()
    mine = chunk(half(full_ref, core), place)
    mine[...] = jnp.concatenate([done_ref[piece] for piece in range(PIECES)], axis=1)
    spread(PLANE - 1, to_all)
    settle(PLANE - 1, to_all)
    back_to_sibling.start()
    back_to_sibling.wait()
    cells = lax.axis_size("slab") * lax.axis_size("sub") * ROWS * ROWS * BRICK
    result_ref[...] = full_ref[:, : TAPS * C] * cells ** (-0.5)


def scratch():
    bf16, f32, dma = jnp.bfloat16, jnp.float32, pltpu.SemaphoreType.DMA
    return [
        pltpu.VMEM((ROWS, ROWS, XC), bf16),
        pltpu.VMEM((ROWS, ROWS, XC), bf16),
        pltpu.VMEM((C, TAPS * C), bf16),
        pltpu.SMEM((ROWS // BRICK, ROWS // BRICK), jnp.int32),
        pltpu.VMEM((ROWS // BRICK, ROWS, XC), f32),
        pltpu.VMEM((ROWS // BRICK, ROWS, XC), bf16),
        pltpu.VMEM((ROWS + 2, 48, PADX), f32),
        pltpu.VMEM((ROWS + 2, 48, PADX), f32),
        pltpu.VMEM((2, ROWS, XC), f32),
        pltpu.VMEM((2, ROWS, XC), f32),
        pltpu.VMEM((2, 48, PADX), f32),
        pltpu.VMEM((3, (ROWS + 2) * ROWS, PADX), bf16),
        pltpu.VMEM((3, (ROWS + 2) * ROWS, PADX), bf16),
        pltpu.VMEM((3, 128, 128 * (ROWS + 2)), bf16),
        pltpu.VMEM((2, 128, 128), bf16),
        pltpu.VMEM((256, 9 * WINDOW), bf16),
        pltpu.VMEM((9 * WINDOW, 256), bf16),
        pltpu.VMEM((3, 384, 256), f32),
        pltpu.VMEM((C, WIDE), f32),
        pltpu.VMEM((2, 2, ROWS, XC), bf16),
        pltpu.VMEM((2, 2, ROWS, XC), bf16),
        pltpu.VMEM((2, 2, ROWS, XC), bf16),
        pltpu.VMEM((2, 2, ROWS, XC), bf16),
        pltpu.VMEM((4, 8, XC), f32),
        pltpu.VMEM((4, 8, XC), f32),
        pltpu.VMEM((HALF, WIDE), f32),
        pltpu.VMEM((HALF, WIDE), f32),
        pltpu.VMEM((PLANE - 1, 8, CHUNK), f32),
        pltpu.VMEM((PIECES, 8, 128), f32),
        pltpu.VMEM((DEEP, 8, 128), f32),
        pltpu.VMEM((PIECES, 8, 128), f32),
        pltpu.VMEM((C, WIDE), f32),
        dma((4,)),
        dma((8,)),
        dma((8,)),
        dma((4,)),
        dma((PLANE - 1,)),
        dma((PLANE - 1,)),
        dma((DEEP - 1,)),
        dma((DEEP - 1,)),
        dma((PIECES - 1,)),
        dma((PIECES - 1,)),
        dma((PLANE - 1,)),
        dma((PLANE - 1,)),
    ]


def deliver_kernel(*refs):
    sources, targets, semaphores = refs[:3], refs[3:6], refs[6]
    copies = [
        pltpu.make_async_copy(source, target, semaphores.at[index])
        for index, (source, target) in enumerate(zip(sources, targets))
    ]
    for copy in copies:
        copy.start()
    for copy in copies:
        copy.wait()


def deliver(*arrays):
    return pl.pallas_call(
        deliver_kernel,
        out_shape=[jax.ShapeDtypeStruct(a.shape, a.dtype) for a in arrays],
        in_specs=[pl.BlockSpec(memory_space=pltpu.VMEM)] * 3,
        out_specs=[pl.BlockSpec(memory_space=pltpu.HBM)] * 3,
        scratch_shapes=[pltpu.SemaphoreType.DMA((3,))],
        compiler_params=pltpu.CompilerParams(vmem_limit_bytes=8 * 2**20),
        cost_estimate=pl.CostEstimate(
            flops=0, bytes_accessed=5 * 2**20, transcendentals=0
        ),
        name="deliver",
    )(*arrays)


def per_device(features, cotangent, weight, occupancy):
    hbm = pl.BlockSpec(memory_space=pltpu.HBM)
    out, grad, total = pl.pallas_call(
        kernel,
        out_shape=[
            pltpu.VMEM(features.shape, jnp.bfloat16),
            pltpu.VMEM(features.shape, jnp.bfloat16),
            pltpu.VMEM((C, TAPS * C), jnp.float32),
        ],
        in_specs=[hbm] * 4,
        out_specs=[pl.BlockSpec(memory_space=pltpu.VMEM)] * 3,
        scratch_shapes=scratch(),
        compiler_params=pltpu.CompilerParams(
            collective_id=0, has_side_effects=True, vmem_limit_bytes=55 * 2**20
        ),
        cost_estimate=pl.CostEstimate(
            flops=11 * 10**9, bytes_accessed=5 * 2**20, transcendentals=0
        ),
        name="convolutions",
    )(features, cotangent, weight, occupancy)
    return deliver(out, grad, total)


def solution(mesh):
    placed = (P("slab", "sub", None), P("slab", "sub", None), P(), P("slab", "sub"))
    return jax.shard_map(
        per_device,
        mesh=mesh,
        in_specs=placed,
        out_specs=(P("slab", "sub", None), P("slab", "sub", None), P()),
        check_vma=False,
    )
```

time: 1070 us -> 52 us (0.05); the launches traced: 1060 us -> 51.8 us
  waiting for transfers between devices: 738 us -> 0 us
  local copies, waits for them, and re-layouts: 240 us -> 0 us
  Pallas kernels: 0 us -> 51.2 us
  matrix products: 33.2 us -> 0 us
  starting transfers between devices: 13.7 us -> 0 us
  between operations: 14.3 us -> 0.64 us
  other arithmetic: 12.7 us -> 0 us
    psum x1 -> x0, waiting for transfers between devices: 734 us -> none  [per_device(): weight_grad = lax.psum(weight_sum, ('slab', 'sub')) * total_cells ** (-0.5)]
    slice x56 -> x0, local copies, waits for them, and re-layouts: 83.1 us -> none  [the longest x24 29.1 us: tap_columns(): grid_cells[shift_z:shift_z + BRICK, shift_y:shift_y + BRICK, shift_x:shif...]
    concatenate x13 -> x0, local copies, waits for them, and re-layouts: 57.6 us -> none  [the longest x12 55.1 us: tap_columns(): return jnp.concatenate(columns, axis=1)]
    pallas_call x0 -> x2, Pallas kernels: none -> 51.2 us  [the longest x1 49.7 us: per_device(): pl.pallas_call(kernel, out_shape=[pltpu.VMEM(features.shape, jnp.bfloat16...]
    another operation x18 -> x0, local copies, waits for them, and re-layouts: 42 us -> none  [the longest x17 41.9 us: per_device(): brick_items = jnp.stack(pieces)]
    dot_general x20 -> x0, matrix products: 33.2 us -> none  [the longest x6 13.5 us: brick_terms(): jnp.dot(grad_cols, weight_back, preferred_element_type=jnp.float32)]
    dynamic_slice x6 -> x0, local copies, waits for them, and re-layouts: 18.9 us -> none  [advance(): lax.dynamic_index_in_dim(brick_items, item_index, 0, keepdims=False)]
    reshape x10 -> x0, local copies, waits for them, and re-layouts: 18.1 us -> none  [the longest x1 6.4 us: per_device(): slot_out.reshape(BZ, BY, 2, BRICK, BRICK, BRICK, C)]
  transfers between devices with their start and end apart: 5 -> 0, of which waited for: 3 -> 0; matrix products, arithmetic and copies ran while one was open for 1% -> 0% of each run, Pallas kernels for 0% -> 0%
where the time goes in v2:
time: 52 us; the launch traced here: 51.8 us
  Pallas kernels  51.2 us (98%)
  between operations  0.64 us (1%)
    pallas_call x1, Pallas kernels, per_device(): pl.pallas_call(kernel, out_shape=[pltpu.VMEM(features.shape, jnp.bfloat16...  49.7 us
    pallas_call x1, Pallas kernels, deliver(): pl.pallas_call(deliver_kernel, out_shape=[jax.ShapeDtypeStruct(a.shape, a...  1.49 us

profile of v2, /device:TPU:1, one launch (start us, length us, event | category | flops | bytes accessed | tf_op | source)
XLA Modules:
  0.0 51.8 jit_solution(16287720627187673401)
XLA Ops:
  0.6 49.7 %convolutions.1 = (bf16[32,32,512]{2,1,0:T(8,128)(2,1)S(1)}, bf16[32,32,512]{2,1,0:T(8,128)(2,1)S(1)}, f32[64,1728]{1,0:T(8,128)S(1)}) custom-call(bf16[32,32,512]{2,1,0:T(8,128)(2,1)} %features_hbm.1, bf16[32,32,512]{2,1,0:T(8,128)(2,1)} %cotangent_hbm.1, bf16[64,1728]{1,0:T(8,128)(2,1)} %weight_hbm.1, s32[4,4]{1,0:T(4,128)} %occ_hbm.1), custom_call_target="tpu_custom_call" | custom-call | flops 11000000512 | bytes 5242880 | tf_op jit(solution)/shard_map/convolutions/pallas_call | solution.py:683
  50.3 1.5 %deliver.1 = (bf16[32,32,512]{2,1,0:T(8,128)(2,1)}, bf16[32,32,512]{2,1,0:T(8,128)(2,1)}, f32[64,1728]{1,0:T(8,128)}) custom-call(bf16[32,32,512]{2,1,0:T(8,128)(2,1)S(1)} %get-tuple-element.6.refs_0_, bf16[32,32,512]{2,1,0:T(8,128)(2,1)S(1)} %get-tuple-element.7.refs_1_, f32[64,1728]{1,0:T(8,128)S(1)} %get-tuple-element.8.refs_2_), custom_call_target="tpu_custom_call" | custom-call | bytes 5242880 | tf_op jit(solution)/shard_map/deliver/pallas_call | solution.py:667

commit v3 on v2

--- a/solution.py
+++ b/solution.py
@@ -18,6 +18,12 @@
 PIECES = 4
 CHUNK = 512
 WIDE = 4 * CHUNK
+PLANE_STEPS = sorted(
+    [(dy, dx) for dy in range(4) for dx in range(4) if dy or dx],
+    key=lambda step: -min(step[0], 4 - step[0]) - min(step[1], 4 - step[1]),
+)
+COLUMN_STEPS = sorted(range(1, DEEP), key=lambda step: -min(step, DEEP - step))
+NEAR_STEPS = (-2, -1, 1)
 HALF = C // 2
 
 FACES_Z = ((1, 0), (-1, 0))
@@ -324,20 +330,17 @@
     lax.fori_loop(0, ROWS, layer, 0)
 
 
-def spread(count, copy):
-    def start(index, _):
-        copy(index).start()
-        return 0
-
-    lax.fori_loop(0, count, start, 0)
-
-
-def settle(count, copy):
-    def wait(index, _):
-        copy(index).wait()
-        return 0
-
-    lax.fori_loop(0, count, wait, 0)
+def start(copies):
+    for copy in copies:
+        copy.start()
+
+
+def arrived(same_bytes, semaphores):
+    pltpu.make_async_copy(same_bytes, same_bytes, semaphores.at[1]).wait()
+
+
+def left(same_bytes, semaphores):
+    pltpu.make_async_copy(same_bytes, same_bytes, semaphores.at[0]).wait()
 
 
 def sibling():
@@ -349,10 +352,10 @@
     return lax.rem(lax.axis_index("slab") // 2, 4) * 4 + lax.axis_index("sub")
 
 
-def plane_partner(index):
-    slab = lax.axis_index("slab")
-    place = lax.rem(plane_place() + index + 1, PLANE)
-    return (slab // 8 * 8 + place // 4 * 2 + lax.rem(slab, 2), lax.rem(place, 4)), place
+def plane_partner(step):
+    slab, sub = lax.axis_index("slab"), lax.axis_index("sub")
+    y, x = lax.rem(slab // 2 + step[0], 4), lax.rem(sub + step[1], 4)
+    return (slab // 8 * 8 + y * 2 + lax.rem(slab, 2), x), y * 4 + x
 
 
 def column_partner(step):
@@ -377,22 +380,30 @@
     def signal(device):
         pl.semaphore_signal(semaphore, inc=1, device_id=device, device_id_type=MESH)
 
-    def plane(index, _):
-        signal(plane_partner(index)[0])
-        return 0
-
-    def column(index, _):
-        signal(column_partner(index + 1)[0])
-        return 0
-
     for direction in DIRECTIONS:
         signal(neighbour(direction))
     signal(sibling())
-    lax.fori_loop(0, PLANE - 1, plane, 0)
-    lax.fori_loop(0, DEEP - 1, column, 0)
+    for step in PLANE_STEPS:
+        signal(plane_partner(step)[0])
+    for step in (1, -1):
+        signal(column_partner(step)[0])
     return lambda: pl.semaphore_wait(
-        semaphore, len(DIRECTIONS) + 1 + (PLANE - 1) + (DEEP - 1)
+        semaphore, len(DIRECTIONS) + 1 + len(PLANE_STEPS) + 2
     )
+
+
+def tell(round_sem, index):
+    for step in (2**index, -(2**index)):
+        pl.semaphore_signal(
+            round_sem.at[index],
+            inc=1,
+            device_id=column_partner(step)[0],
+            device_id_type=MESH,
+        )
+
+
+def hear(round_sem, index):
+    pl.semaphore_wait(round_sem.at[index], 2)
 
 
 def kernel(
@@ -439,14 +450,11 @@
     halo_send_sem,
     halo_recv_sem,
     core_sem,
-    plane_send_sem,
-    plane_recv_sem,
-    column_send_sem,
-    column_recv_sem,
-    near_send_sem,
-    near_recv_sem,
-    gather_send_sem,
-    gather_recv_sem,
+    plane_sem,
+    column_sem,
+    near_sem,
+    gather_sem,
+    round_sem,
 ):
     loads = [
         pltpu.make_async_copy(features_hbm, features_ref, load_sem.at[0]),
@@ -468,50 +476,56 @@
         device_id_type=MESH,
     )
 
-    def to_plane(index):
-        device, other = plane_partner(index)
-        return pltpu.make_async_remote_copy(
-            src_ref=chunk(half_ref, other),
-            dst_ref=plane_recv.at[index],
-            send_sem=plane_send_sem.at[index],
-            recv_sem=plane_recv_sem.at[index],
-            device_id=device,
-            device_id_type=MESH,
-        )
-
-    def to_column(index):
-        device, other = column_partner(index + 1)
-        return pltpu.make_async_remote_copy(
-            src_ref=pieces_ref.at[lax.rem(other, PIECES)],
-            dst_ref=column_recv.at[z],
-            send_sem=column_send_sem.at[index],
-            recv_sem=column_recv_sem.at[index],
-            device_id=device,
-            device_id_type=MESH,
-        )
-
-    def to_near(index):
-        device, _ = column_partner((-1, 1, -2)[index])
-        return pltpu.make_async_remote_copy(
+    mine = chunk(half(full_ref, core), place)
+    to_plane, to_all = [], []
+    for index, step in enumerate(PLANE_STEPS):
+        device, other = plane_partner(step)
+        to_plane.append(
+            pltpu.make_async_remote_copy(
+                src_ref=chunk(half_ref, other),
+                dst_ref=plane_recv.at[index],
+                send_sem=plane_sem.at[0],
+                recv_sem=plane_sem.at[1],
+                device_id=device,
+                device_id_type=MESH,
+            )
+        )
+        to_all.append(
+            pltpu.make_async_remote_copy(
+                src_ref=mine,
+                dst_ref=mine,
+                send_sem=gather_sem.at[0],
+                recv_sem=gather_sem.at[1],
+                device_id=device,
+                device_id_type=MESH,
+            )
+        )
+    to_column = []
+    for step in COLUMN_STEPS:
+        device, other = column_partner(step)
+        to_column.append(
+            pltpu.make_async_remote_copy(
+                src_ref=pieces_ref.at[lax.rem(other, PIECES)],
+                dst_ref=column_recv.at[z],
+                send_sem=column_sem.at[0],
+                recv_sem=column_sem.at[1],
+                device_id=device,
+                device_id_type=MESH,
+            )
+        )
+    to_near = [
+        pltpu.make_async_remote_copy(
             src_ref=done_ref.at[own],
             dst_ref=done_ref.at[own],
-            send_sem=near_send_sem.at[index],
-            recv_sem=near_recv_sem.at[index],
-            device_id=device,
+            send_sem=near_sem.at[0],
+            recv_sem=near_sem.at[1],
+            device_id=column_partner(step)[0],
             device_id_type=MESH,
         )
-
-    def to_all(index):
-        device, _ = plane_partner(index)
-        mine = chunk(half(full_ref, core), place)
-        return pltpu.make_async_remote_copy(
-            src_ref=mine,
-            dst_ref=mine,
-            send_sem=gather_send_sem.at[index],
-            recv_sem=gather_recv_sem.at[index],
-            device_id=device,
-            device_id_type=MESH,
-        )
+        for step in NEAR_STEPS
+    ]
+    column_bytes = column_recv.at[pl.ds(0, DEEP - 1)]
+    near_bytes = done_ref.at[pl.ds(0, PIECES - 1)]
 
     back_to_sibling = pltpu.make_async_remote_copy(
         src_ref=half(full_ref, core),
@@ -535,12 +549,15 @@
     everyone_here()
     for copy in halos:
         copy.start()
+    tell(round_sem, 0)
 
     prepare_both(features_ref, cotangent_ref, narrow_ref, shifted_in, turned_ref)
     for side in range(2):
         edge_turned_ref[side] = pairs(edge_grad[side]).T.astype(jnp.bfloat16)
     inner_gradient(turned_ref, shifted_in, product_ref)
 
+    hear(round_sem, 0)
+    tell(round_sem, 1)
     for copy in halos:
         copy.wait()
     place_layers(0, buffers, padded_in)
@@ -555,19 +572,22 @@
     build_weights(weight_ref, forward_ref, backward_ref)
     pad_rows(shifted_in, padded_in)
     to_sibling.wait()
+    hear(round_sem, 1)
+    tell(round_sem, 2)
     half_ref[...] = half(share_ref, core)[...] + core_recv[...]
-    spread(PLANE - 1, to_plane)
+    start(to_plane)
 
     place_rows(stage_ref, padded_in)
     shift_rows(padded_in, shifted_in)
     convolve(shifted_in, forward_ref, True, mask_ref, out_ref, 0, 3)
-    settle(PLANE - 1, to_plane)
+    arrived(plane_recv, plane_sem)
     total = chunk(half_ref, place)[...]
     for index in range(PLANE - 1):
         total = total + plane_recv[index]
     for piece in range(PIECES):
         pieces_ref[piece] = total[:, 128 * piece : 128 * piece + 128]
-    spread(DEEP - 1, to_column)
+    hear(round_sem, 2)
+    start(to_column)
 
     convolve(shifted_in, forward_ref, True, mask_ref, out_ref, 3, 4)
     prepare(cotangent_ref, narrow_ref, shifted_grad)
@@ -579,23 +599,24 @@
     for layer in (0, ROWS + 1):
         shift_layer(padded_grad, shifted_grad, layer, (0, 1, 2))
     convolve(shifted_grad, backward_ref, False, mask_ref, grad_ref, 0, 2)
-    settle(DEEP - 1, to_column)
+    arrived(column_bytes, column_sem)
     column_recv[z] = pieces_ref[own]
     piece = column_recv[0]
     for index in range(1, DEEP):
         piece = piece + column_recv[index]
     done_ref[own] = piece
-    for index in range(PIECES - 1):
-        to_near(index).start()
+    start(to_near)
 
     convolve(shifted_grad, backward_ref, False, mask_ref, grad_ref, 2, 4)
-    for index in range(PIECES - 1):
-        to_near(index).wait()
-    mine = chunk(half(full_ref, core), place)
+    arrived(near_bytes, near_sem)
     mine[...] = jnp.concatenate([done_ref[piece] for piece in range(PIECES)], axis=1)
-    spread(PLANE - 1, to_all)
-    settle(PLANE - 1, to_all)
+    start(to_all)
+    arrived(plane_recv, gather_sem)
     back_to_sibling.start()
+    left(plane_recv, plane_sem)
+    left(column_bytes, column_sem)
+    left(near_bytes, near_sem)
+    left(plane_recv, gather_sem)
     back_to_sibling.wait()
     cells = lax.axis_size("slab") * lax.axis_size("sub") * ROWS * ROWS * BRICK
     result_ref[...] = full_ref[:, : TAPS * C] * cells ** (-0.5)
@@ -640,14 +661,11 @@
         dma((8,)),
         dma((8,)),
         dma((4,)),
-        dma((PLANE - 1,)),
-        dma((PLANE - 1,)),
-        dma((DEEP - 1,)),
-        dma((DEEP - 1,)),
-        dma((PIECES - 1,)),
-        dma((PIECES - 1,)),
-        dma((PLANE - 1,)),
-        dma((PLANE - 1,)),
+        dma((2,)),
+        dma((2,)),
+        dma((2,)),
+        dma((2,)),
+        pltpu.SemaphoreType.REGULAR((3,)),
     ]
 
 

time: 52 us -> 48.8 us (0.938)
  Pallas kernels: 51.2 us -> 48.1 us
    pallas_call x1, Pallas kernels: 49.7 us -> 46.6 us  [per_device(): pl.pallas_call(kernel, out_shape=[pltpu.VMEM(features.shape, jnp.bfloat16...]
where the time goes in v3:
time: 48.8 us; the launch traced here: 48.7 us
  Pallas kernels  48.1 us (99%)
  between operations  0.64 us (1%)
    pallas_call x1, Pallas kernels, per_device(): pl.pallas_call(kernel, out_shape=[pltpu.VMEM(features.shape, jnp.bfloat16...  46.6 us
    pallas_call x1, Pallas kernels, deliver(): pl.pallas_call(deliver_kernel, out_shape=[jax.ShapeDtypeStruct(a.shape, a...  1.49 us

profile of v3, /device:TPU:1, one launch (start us, length us, event | category | flops | bytes accessed | tf_op | source)
XLA Modules:
  0.0 48.7 jit_solution(1903194046246535091)
XLA Ops:
  0.6 46.6 %convolutions.1 = (bf16[32,32,512]{2,1,0:T(8,128)(2,1)S(1)}, bf16[32,32,512]{2,1,0:T(8,128)(2,1)S(1)}, f32[64,1728]{1,0:T(8,128)S(1)}) custom-call(bf16[32,32,512]{2,1,0:T(8,128)(2,1)} %features_hbm.1, bf16[32,32,512]{2,1,0:T(8,128)(2,1)} %cotangent_hbm.1, bf16[64,1728]{1,0:T(8,128)(2,1)} %weight_hbm.1, s32[4,4]{1,0:T(4,128)} %occ_hbm.1), custom_call_target="tpu_custom_call" | custom-call | flops 11000000512 | bytes 5242880 | tf_op jit(solution)/shard_map/convolutions/pallas_call | solution.py:701
  47.2 1.5 %deliver.1 = (bf16[32,32,512]{2,1,0:T(8,128)(2,1)}, bf16[32,32,512]{2,1,0:T(8,128)(2,1)}, f32[64,1728]{1,0:T(8,128)}) custom-call(bf16[32,32,512]{2,1,0:T(8,128)(2,1)S(1)} %get-tuple-element.6.refs_0_, bf16[32,32,512]{2,1,0:T(8,128)(2,1)S(1)} %get-tuple-element.7.refs_1_, f32[64,1728]{1,0:T(8,128)S(1)} %get-tuple-element.8.refs_2_), custom_call_target="tpu_custom_call" | custom-call | bytes 5242880 | tf_op jit(solution)/shard_map/deliver/pallas_call | solution.py:685

commit v4 on v3

--- a/solution.py
+++ b/solution.py
@@ -22,8 +22,18 @@
     [(dy, dx) for dy in range(4) for dx in range(4) if dy or dx],
     key=lambda step: -min(step[0], 4 - step[0]) - min(step[1], 4 - step[1]),
 )
+PLANE_ROUNDS = (((0, 1), (0, 3), (1, 0), (3, 0)), ((1, 1), (1, 3), (3, 1), (3, 3)))
 COLUMN_STEPS = sorted(range(1, DEEP), key=lambda step: -min(step, DEEP - step))
-NEAR_STEPS = (-2, -1, 1)
+NEAR_STEPS = sorted(
+    [
+        (dz, dy, dx)
+        for dz in (-2, -1, 0, 1)
+        for dy in range(4)
+        for dx in range(4)
+        if dz or dy or dx
+    ],
+    key=lambda step: -abs(step[0]) - min(step[1], 4 - step[1]) - min(step[2], 4 - step[2]),
+)
 HALF = C // 2
 
 FACES_Z = ((1, 0), (-1, 0))
@@ -131,24 +141,21 @@
     lax.fori_loop(0, ROWS, layer, 0, unroll=unroll)
 
 
-def prepare_both(features_ref, cotangent_ref, narrow_ref, shifted_ref, turned_ref):
+def prepare_both(features_ref, cotangent_ref, narrow_ref, shifted_ref, turned_ref, layers):
     edge = jnp.zeros((128, 1), jnp.bfloat16)
     row = lax.broadcasted_iota(jnp.int32, (128, 128), 1) % ROWS
     not_last = (row != ROWS - 1).astype(jnp.float32).astype(jnp.bfloat16)
     not_first = (row != 0).astype(jnp.float32).astype(jnp.bfloat16)
-
-    def layer(z, _):
+    for z in layers:
         mask = narrow_ref[z // BRICK]
-        rows = pl.ds(pl.multiple_of((z + 1) * ROWS, ROWS), ROWS)
-        shifted_ref[1, rows, :] = widen(features_ref[z] * mask)
-        column = pl.ds(pl.multiple_of(128 * (z + 1), 128), 128)
+        shifted_ref[1, ROWS * (z + 1) : ROWS * (z + 2), :] = widen(features_ref[z] * mask)
+        column = slice(128 * (z + 1), 128 * (z + 2))
         turned = pairs(cotangent_ref[z] * mask).T
-        turned_ref[0, :, column] = not_last * jnp.concatenate([turned[:, 1:], edge], axis=1)
+        down = jnp.concatenate([turned[:, 1:], edge], axis=1)
+        up = jnp.concatenate([edge, turned[:, :127]], axis=1)
+        turned_ref[0, :, column] = not_last * down
         turned_ref[1, :, column] = turned
-        turned_ref[2, :, column] = not_first * jnp.concatenate([edge, turned[:, :127]], axis=1)
-        return 0
-
-    lax.fori_loop(0, ROWS, layer, 0, unroll=8)
+        turned_ref[2, :, column] = not_first * up
 
 
 def pad_rows(shifted_ref, padded_ref):
@@ -174,24 +181,30 @@
     lax.fori_loop(1, ROWS + 1, layer, 0, unroll=8)
 
 
-def inner_gradient(turned_ref, shifted_ref, product_ref):
+def inner_gradient(turned_ref, shifted_ref, product_ref, first, last):
     window = jnp.concatenate(
         [
             shifted_ref[1, ROWS * z : ROWS * z + ROWS, 128 * p : 128 * p + 256]
-            for z in range(1, ROWS + 1)
+            for z in range(first + 1, last + 1)
             for p in range(4)
         ],
         axis=0,
     )
     for b in range(3):
         turned = jnp.concatenate(
-            [turned_ref[b, :, 128 * (2 - a) : 128 * (2 - a + ROWS)] for a in range(3)],
+            [
+                turned_ref[b, :, 128 * (first + 2 - a) : 128 * (last + 2 - a)]
+                for a in range(3)
+            ],
             axis=0,
         )
-        product_ref[b] = jnp.dot(turned, window, preferred_element_type=jnp.float32)
-
-
-def outer_gradient(turned_ref, shifted_ref, edge_turned_ref, stage_ref, product_ref, share_ref):
+        product = jnp.dot(turned, window, preferred_element_type=jnp.float32)
+        if first > 0:
+            product = product_ref[b] + product
+        product_ref[b] = product
+
+
+def outer_gradient(turned_ref, shifted_ref, edge_turned_ref, stage_ref, product_ref, share_ref, done):
     def along_z(z, layer):
         first = ROWS * layer
         window = jnp.concatenate(
@@ -213,8 +226,8 @@
 
     low_z, high_z = along_z(0, 0), along_z(ROWS - 1, ROWS + 1)
     edges = {0: along_y(0), 2: along_y(1)}
-    for b in range(3):
-        for a in range(3):
+    for a in range(3):
+        for b in range(3):
             term = product_ref[b, 128 * a : 128 * a + 128, :]
             if a == 0:
                 term = term + low_z[:, 256 * b : 256 * b + 256]
@@ -226,6 +239,7 @@
             share_ref[:, 192 * ab : 192 * ab + 192] = (
                 term[:C, :192] + term[C:, C : C + 192]
             )
+        done(a)
 
 
 def convolve(shifted_ref, weight_ref, transposed, mask_ref, out_ref, start, stop, layers=BRICK):
@@ -364,12 +378,24 @@
     return (z * 8 + lax.rem(slab, 8), lax.axis_index("sub")), z
 
 
+def block_partner(step):
+    (slab, sub), _ = plane_partner(step[1:])
+    z = lax.rem(slab // 8 + step[0] + DEEP, DEEP)
+    return z * 8 + lax.rem(slab, 8), sub
+
+
 def chunk(ref, place):
     row = pl.multiple_of(place // 4 * 8, 8)
     lane = pl.multiple_of(lax.rem(place, 4) * CHUNK, CHUNK)
     return ref.at[pl.ds(row, 8), pl.ds(lane, CHUNK)]
 
 
+def tile(ref, place, piece):
+    row = pl.multiple_of(place // 4 * 8, 8)
+    lane = pl.multiple_of(lax.rem(place, 4) * CHUNK + piece * 128, 128)
+    return ref.at[pl.ds(row, 8), pl.ds(lane, 128)]
+
+
 def half(ref, core):
     return ref.at[pl.ds(pl.multiple_of(core * HALF, HALF), HALF)]
 
@@ -383,13 +409,25 @@
     for direction in DIRECTIONS:
         signal(neighbour(direction))
     signal(sibling())
-    for step in PLANE_STEPS:
+    for step in ((1, 0), (3, 0)):
         signal(plane_partner(step)[0])
     for step in (1, -1):
         signal(column_partner(step)[0])
-    return lambda: pl.semaphore_wait(
-        semaphore, len(DIRECTIONS) + 1 + len(PLANE_STEPS) + 2
-    )
+    return lambda: pl.semaphore_wait(semaphore, len(DIRECTIONS) + 1 + 2 + 2)
+
+
+def tell_plane(plane_round_sem, index):
+    for step in PLANE_ROUNDS[index]:
+        pl.semaphore_signal(
+            plane_round_sem.at[index],
+            inc=1,
+            device_id=plane_partner(step)[0],
+            device_id_type=MESH,
+        )
+
+
+def hear_plane(plane_round_sem, index):
+    pl.semaphore_wait(plane_round_sem.at[index], len(PLANE_ROUNDS[index]))
 
 
 def tell(round_sem, index):
@@ -444,7 +482,7 @@
     plane_recv,
     pieces_ref,
     column_recv,
-    done_ref,
+    gather_bytes,
     full_ref,
     load_sem,
     halo_send_sem,
@@ -452,9 +490,9 @@
     core_sem,
     plane_sem,
     column_sem,
-    near_sem,
     gather_sem,
     round_sem,
+    plane_round_sem,
 ):
     loads = [
         pltpu.make_async_copy(features_hbm, features_ref, load_sem.at[0]),
@@ -467,16 +505,19 @@
     own = lax.rem(z, PIECES)
     buffers = (face_send, face_recv, edge_send, edge_recv, corner_send, corner_recv)
     halos = halo_copies(buffers, halo_send_sem, halo_recv_sem)
-    to_sibling = pltpu.make_async_remote_copy(
-        src_ref=half(share_ref, 1 - core),
-        dst_ref=core_recv,
-        send_sem=core_sem.at[0],
-        recv_sem=core_sem.at[1],
-        device_id=sibling(),
-        device_id_type=MESH,
-    )
-
-    mine = chunk(half(full_ref, core), place)
+    lanes = (0, 512, 1152, WIDE)
+    to_sibling = [
+        pltpu.make_async_remote_copy(
+            src_ref=half(share_ref, 1 - core).at[:, lanes[a] : lanes[a + 1]],
+            dst_ref=core_recv.at[:, lanes[a] : lanes[a + 1]],
+            send_sem=core_sem.at[0],
+            recv_sem=core_sem.at[1],
+            device_id=sibling(),
+            device_id_type=MESH,
+        )
+        for a in range(3)
+    ]
+    mine = tile(half(full_ref, core), place, own)
     to_plane, to_all = [], []
     for index, step in enumerate(PLANE_STEPS):
         device, other = plane_partner(step)
@@ -490,13 +531,14 @@
                 device_id_type=MESH,
             )
         )
+    for step in NEAR_STEPS:
         to_all.append(
             pltpu.make_async_remote_copy(
                 src_ref=mine,
                 dst_ref=mine,
                 send_sem=gather_sem.at[0],
                 recv_sem=gather_sem.at[1],
-                device_id=device,
+                device_id=block_partner(step),
                 device_id_type=MESH,
             )
         )
@@ -513,19 +555,7 @@
                 device_id_type=MESH,
             )
         )
-    to_near = [
-        pltpu.make_async_remote_copy(
-            src_ref=done_ref.at[own],
-            dst_ref=done_ref.at[own],
-            send_sem=near_sem.at[0],
-            recv_sem=near_sem.at[1],
-            device_id=column_partner(step)[0],
-            device_id_type=MESH,
-        )
-        for step in NEAR_STEPS
-    ]
     column_bytes = column_recv.at[pl.ds(0, DEEP - 1)]
-    near_bytes = done_ref.at[pl.ds(0, PIECES - 1)]
 
     back_to_sibling = pltpu.make_async_remote_copy(
         src_ref=half(full_ref, core),
@@ -550,14 +580,21 @@
     for copy in halos:
         copy.start()
     tell(round_sem, 0)
-
-    prepare_both(features_ref, cotangent_ref, narrow_ref, shifted_in, turned_ref)
+    tell_plane(plane_round_sem, 0)
+
+    raw_refs = (features_ref, cotangent_ref)
+    middle = ROWS // 2
+    prepare_both(*raw_refs, narrow_ref, shifted_in, turned_ref, range(middle + 1))
+    prepare_both(*raw_refs, narrow_ref, shifted_in, turned_ref, range(middle + 1, ROWS))
+    inner_gradient(turned_ref, shifted_in, product_ref, 0, middle)
     for side in range(2):
         edge_turned_ref[side] = pairs(edge_grad[side]).T.astype(jnp.bfloat16)
-    inner_gradient(turned_ref, shifted_in, product_ref)
+    inner_gradient(turned_ref, shifted_in, product_ref, middle, ROWS)
 
     hear(round_sem, 0)
     tell(round_sem, 1)
+    hear_plane(plane_round_sem, 0)
+    tell_plane(plane_round_sem, 1)
     for copy in halos:
         copy.wait()
     place_layers(0, buffers, padded_in)
@@ -565,16 +602,22 @@
         shift_layer(padded_in, shifted_in, layer, (0, 1, 2))
     stage_edges(0, buffers, stage_ref)
     outer_gradient(
-        turned_ref, shifted_in, edge_turned_ref, stage_ref, product_ref, share_ref
+        turned_ref,
+        shifted_in,
+        edge_turned_ref,
+        stage_ref,
+        product_ref,
+        share_ref,
+        lambda a: to_sibling[a].start(),
     )
-    to_sibling.start()
 
     build_weights(weight_ref, forward_ref, backward_ref)
     pad_rows(shifted_in, padded_in)
-    to_sibling.wait()
+    pltpu.make_async_copy(core_recv, core_recv, core_sem.at[1]).wait()
     hear(round_sem, 1)
     tell(round_sem, 2)
     half_ref[...] = half(share_ref, core)[...] + core_recv[...]
+    hear_plane(plane_round_sem, 1)
     start(to_plane)
 
     place_rows(stage_ref, padded_in)
@@ -604,19 +647,16 @@
     piece = column_recv[0]
     for index in range(1, DEEP):
         piece = piece + column_recv[index]
-    done_ref[own] = piece
-    start(to_near)
+    mine[...] = piece
+    start(to_all)
 
     convolve(shifted_grad, backward_ref, False, mask_ref, grad_ref, 2, 4)
-    arrived(near_bytes, near_sem)
-    mine[...] = jnp.concatenate([done_ref[piece] for piece in range(PIECES)], axis=1)
-    start(to_all)
-    arrived(plane_recv, gather_sem)
+    arrived(gather_bytes, gather_sem)
     back_to_sibling.start()
+    left(core_recv, core_sem)
     left(plane_recv, plane_sem)
     left(column_bytes, column_sem)
-    left(near_bytes, near_sem)
-    left(plane_recv, gather_sem)
+    left(gather_bytes, gather_sem)
     back_to_sibling.wait()
     cells = lax.axis_size("slab") * lax.axis_size("sub") * ROWS * ROWS * BRICK
     result_ref[...] = full_ref[:, : TAPS * C] * cells ** (-0.5)
@@ -655,7 +695,7 @@
         pltpu.VMEM((PLANE - 1, 8, CHUNK), f32),
         pltpu.VMEM((PIECES, 8, 128), f32),
         pltpu.VMEM((DEEP, 8, 128), f32),
-        pltpu.VMEM((PIECES, 8, 128), f32),
+        pltpu.VMEM((len(NEAR_STEPS), 8, 128), f32),
         pltpu.VMEM((C, WIDE), f32),
         dma((4,)),
         dma((8,)),
@@ -664,8 +704,8 @@
         dma((2,)),
         dma((2,)),
         dma((2,)),
-        dma((2,)),
         pltpu.SemaphoreType.REGULAR((3,)),
+        pltpu.SemaphoreType.REGULAR((2,)),
     ]
 
 

time: 48.8 us -> 46.5 us (0.953)
  Pallas kernels: 48.1 us -> 45.8 us
    pallas_call x1, Pallas kernels: 46.6 us -> 44.3 us  [per_device(): pl.pallas_call(kernel, out_shape=[pltpu.VMEM(features.shape, jnp.bfloat16...]
where the time goes in v4:
time: 46.5 us; the launch traced here: 46.4 us
  Pallas kernels  45.8 us (98%)
  between operations  0.64 us (1%)
    pallas_call x1, Pallas kernels, per_device(): pl.pallas_call(kernel, out_shape=[pltpu.VMEM(features.shape, jnp.bfloat16...  44.3 us
    pallas_call x1, Pallas kernels, deliver(): pl.pallas_call(deliver_kernel, out_shape=[jax.ShapeDtypeStruct(a.shape, a...  1.49 us

profile of v4, /device:TPU:1, one launch (start us, length us, event | category | flops | bytes accessed | tf_op | source)
XLA Modules:
  0.0 46.4 jit_solution(10292654496402770247)
XLA Ops:
  0.6 44.3 %convolutions.1 = (bf16[32,32,512]{2,1,0:T(8,128)(2,1)S(1)}, bf16[32,32,512]{2,1,0:T(8,128)(2,1)S(1)}, f32[64,1728]{1,0:T(8,128)S(1)}) custom-call(bf16[32,32,512]{2,1,0:T(8,128)(2,1)} %features_hbm.1, bf16[32,32,512]{2,1,0:T(8,128)(2,1)} %cotangent_hbm.1, bf16[64,1728]{1,0:T(8,128)(2,1)} %weight_hbm.1, s32[4,4]{1,0:T(4,128)} %occ_hbm.1), custom_call_target="tpu_custom_call" | custom-call | flops 11000000512 | bytes 5242880 | tf_op jit(solution)/shard_map/convolutions/pallas_call | solution.py:741
  44.9 1.5 %deliver.1 = (bf16[32,32,512]{2,1,0:T(8,128)(2,1)}, bf16[32,32,512]{2,1,0:T(8,128)(2,1)}, f32[64,1728]{1,0:T(8,128)}) custom-call(bf16[32,32,512]{2,1,0:T(8,128)(2,1)S(1)} %get-tuple-element.6.refs_0_, bf16[32,32,512]{2,1,0:T(8,128)(2,1)S(1)} %get-tuple-element.7.refs_1_, f32[64,1728]{1,0:T(8,128)S(1)} %get-tuple-element.8.refs_2_), custom_call_target="tpu_custom_call" | custom-call | bytes 5242880 | tf_op jit(solution)/shard_map/deliver/pallas_call | solution.py:725

commit v5 on v4

--- a/solution.py
+++ b/solution.py
@@ -294,25 +294,30 @@
 
 def halo_copies(buffers, send_sem, recv_sem):
     face_send, face_recv, edge_send, edge_recv, corner_send, corner_recv = buffers
-    copies = []
-    for index, direction in enumerate(DIRECTIONS):
-        if index < 2:
-            source, target = face_send.at[index], face_recv.at[index]
-        elif index < 4:
-            source, target = edge_send.at[index - 2], edge_recv.at[index - 2]
-        else:
-            source, target = corner_send.at[index - 4], corner_recv.at[index - 4]
-        copies.append(
-            pltpu.make_async_remote_copy(
-                src_ref=source,
-                dst_ref=target,
-                send_sem=send_sem.at[index],
-                recv_sem=recv_sem.at[index],
-                device_id=neighbour(direction),
-                device_id_type=MESH,
-            )
-        )
-    return copies
+    pieces = [
+        (direction, corner_send.at[index], corner_recv.at[index])
+        for index, direction in enumerate(CORNERS)
+    ]
+    for tensor in range(2):
+        for directions, source, target in (
+            (FACES_Z, face_send, face_recv),
+            (FACES_Y, edge_send, edge_recv),
+        ):
+            for index, direction in enumerate(directions):
+                pieces.append(
+                    (direction, source.at[index, tensor], target.at[index, tensor])
+                )
+    return [
+        pltpu.make_async_remote_copy(
+            src_ref=source,
+            dst_ref=target,
+            send_sem=send_sem.at[index],
+            recv_sem=recv_sem.at[index],
+            device_id=neighbour(direction),
+            device_id_type=MESH,
+        )
+        for index, (direction, source, target) in enumerate(pieces)
+    ]
 
 
 def place_layers(tensor, buffers, padded_ref):
@@ -595,8 +600,8 @@
     tell(round_sem, 1)
     hear_plane(plane_round_sem, 0)
     tell_plane(plane_round_sem, 1)
-    for copy in halos:
-        copy.wait()
+    for copy in halos[:8]:
+        copy.wait_recv()
     place_layers(0, buffers, padded_in)
     for layer in (0, ROWS + 1):
         shift_layer(padded_in, shifted_in, layer, (0, 1, 2))
@@ -635,6 +640,10 @@
     convolve(shifted_in, forward_ref, True, mask_ref, out_ref, 3, 4)
     prepare(cotangent_ref, narrow_ref, shifted_grad)
     pad_rows(shifted_grad, padded_grad)
+    for copy in halos[8:]:
+        copy.wait_recv()
+    for copy in halos:
+        copy.wait_send()
     place_layers(1, buffers, padded_grad)
     stage_edges(1, buffers, stage_ref)
     place_rows(stage_ref, padded_grad)
@@ -698,8 +707,8 @@
         pltpu.VMEM((len(NEAR_STEPS), 8, 128), f32),
         pltpu.VMEM((C, WIDE), f32),
         dma((4,)),
-        dma((8,)),
-        dma((8,)),
+        dma((12,)),
+        dma((12,)),
         dma((4,)),
         dma((2,)),
         dma((2,)),

time: 46.5 us -> 45.9 us (0.987)
  Pallas kernels: 45.8 us -> 45.1 us
    pallas_call x1, Pallas kernels: 44.3 us -> 43.6 us  [per_device(): pl.pallas_call(kernel, out_shape=[pltpu.VMEM(features.shape, jnp.bfloat16...]
where the time goes in v5:
time: 45.9 us; the launch traced here: 45.8 us
  Pallas kernels  45.1 us (98%)
  between operations  0.64 us (1%)
    pallas_call x1, Pallas kernels, per_device(): pl.pallas_call(kernel, out_shape=[pltpu.VMEM(features.shape, jnp.bfloat16...  43.6 us
    pallas_call x1, Pallas kernels, deliver(): pl.pallas_call(deliver_kernel, out_shape=[jax.ShapeDtypeStruct(a.shape, a...  1.49 us

profile of v5, /device:TPU:1, one launch (start us, length us, event | category | flops | bytes accessed | tf_op | source)
XLA Modules:
  0.0 45.8 jit_solution(14920163552466170762)
XLA Ops:
  0.6 43.6 %convolutions.1 = (bf16[32,32,512]{2,1,0:T(8,128)(2,1)S(1)}, bf16[32,32,512]{2,1,0:T(8,128)(2,1)S(1)}, f32[64,1728]{1,0:T(8,128)S(1)}) custom-call(bf16[32,32,512]{2,1,0:T(8,128)(2,1)} %features_hbm.1, bf16[32,32,512]{2,1,0:T(8,128)(2,1)} %cotangent_hbm.1, bf16[64,1728]{1,0:T(8,128)(2,1)} %weight_hbm.1, s32[4,4]{1,0:T(4,128)} %occ_hbm.1), custom_call_target="tpu_custom_call" | custom-call | flops 11000000512 | bytes 5242880 | tf_op jit(solution)/shard_map/convolutions/pallas_call | solution.py:750
  44.3 1.5 %deliver.1 = (bf16[32,32,512]{2,1,0:T(8,128)(2,1)}, bf16[32,32,512]{2,1,0:T(8,128)(2,1)}, f32[64,1728]{1,0:T(8,128)}) custom-call(bf16[32,32,512]{2,1,0:T(8,128)(2,1)S(1)} %get-tuple-element.6.refs_0_, bf16[32,32,512]{2,1,0:T(8,128)(2,1)S(1)} %get-tuple-element.7.refs_1_, f32[64,1728]{1,0:T(8,128)S(1)} %get-tuple-element.8.refs_2_), custom_call_target="tpu_custom_call" | custom-call | bytes 5242880 | tf_op jit(solution)/shard_map/deliver/pallas_call | solution.py:734

commit v6 on v5

--- a/solution.py
+++ b/solution.py
@@ -411,7 +411,7 @@
     def signal(device):
         pl.semaphore_signal(semaphore, inc=1, device_id=device, device_id_type=MESH)
 
-    for direction in DIRECTIONS:
+    for direction in CORNERS + FACES_Z + FACES_Y:
         signal(neighbour(direction))
     signal(sibling())
     for step in ((1, 0), (3, 0)):
@@ -502,8 +502,8 @@
     loads = [
         pltpu.make_async_copy(features_hbm, features_ref, load_sem.at[0]),
         pltpu.make_async_copy(cotangent_hbm, cotangent_ref, load_sem.at[1]),
-        pltpu.make_async_copy(weight_hbm, weight_ref, load_sem.at[2]),
     ]
+    weight_load = pltpu.make_async_copy(weight_hbm, weight_ref, load_sem.at[2])
     flags = pltpu.make_async_copy(occ_hbm, occ_ref, load_sem.at[3])
     slab = lax.axis_index("slab")
     z, core, place = slab // 8, lax.rem(slab, 2), plane_place()
@@ -584,6 +584,7 @@
     everyone_here()
     for copy in halos:
         copy.start()
+    weight_load.start()
     tell(round_sem, 0)
     tell_plane(plane_round_sem, 0)
 
@@ -616,6 +617,7 @@
         lambda a: to_sibling[a].start(),
     )
 
+    weight_load.wait()
     build_weights(weight_ref, forward_ref, backward_ref)
     pad_rows(shifted_in, padded_in)
     pltpu.make_async_copy(core_recv, core_recv, core_sem.at[1]).wait()

time: 45.9 us -> 45.8 us (level)
  no operation moved by 1% of the time
where the time goes in v6:
time: 45.8 us; the launch traced here: 45.6 us
  Pallas kernels  45 us (98%)
  between operations  0.64 us (1%)
    pallas_call x1, Pallas kernels, per_device(): pl.pallas_call(kernel, out_shape=[pltpu.VMEM(features.shape, jnp.bfloat16...  43.5 us
    pallas_call x1, Pallas kernels, deliver(): pl.pallas_call(deliver_kernel, out_shape=[jax.ShapeDtypeStruct(a.shape, a...  1.49 us

profile of v6, /device:TPU:1, one launch (start us, length us, event | category | flops | bytes accessed | tf_op | source)
XLA Modules:
  0.0 45.6 jit_solution(1769173355213722597)
XLA Ops:
  0.6 43.5 %convolutions.1 = (bf16[32,32,512]{2,1,0:T(8,128)(2,1)S(1)}, bf16[32,32,512]{2,1,0:T(8,128)(2,1)S(1)}, f32[64,1728]{1,0:T(8,128)S(1)}) custom-call(bf16[32,32,512]{2,1,0:T(8,128)(2,1)} %features_hbm.1, bf16[32,32,512]{2,1,0:T(8,128)(2,1)} %cotangent_hbm.1, bf16[64,1728]{1,0:T(8,128)(2,1)} %weight_hbm.1, s32[4,4]{1,0:T(4,128)} %occ_hbm.1), custom_call_target="tpu_custom_call" | custom-call | flops 11000000512 | bytes 5242880 | tf_op jit(solution)/shard_map/convolutions/pallas_call | solution.py:752
  44.1 1.5 %deliver.1 = (bf16[32,32,512]{2,1,0:T(8,128)(2,1)}, bf16[32,32,512]{2,1,0:T(8,128)(2,1)}, f32[64,1728]{1,0:T(8,128)}) custom-call(bf16[32,32,512]{2,1,0:T(8,128)(2,1)S(1)} %get-tuple-element.6.refs_0_, bf16[32,32,512]{2,1,0:T(8,128)(2,1)S(1)} %get-tuple-element.7.refs_1_, f32[64,1728]{1,0:T(8,128)S(1)} %get-tuple-element.8.refs_2_), custom_call_target="tpu_custom_call" | custom-call | bytes 5242880 | tf_op jit(solution)/shard_map/deliver/pallas_call | solution.py:736
